TPU v7x, 32 devices: a whole 2x2x4 slice. The times are simulated.
32 devices in a mesh: groups: 2 (over y), row: 4 (over z), col: 2 (over x), chan: 2 (over core).
Axes of the slice: x: 2, y: 2, z: 4, core: 2. Of those that a mesh axis runs over, the one named last changes fastest.
Arguments:
- layer_input: bfloat16 [2, 64, 32, 512], P(None, None, ('groups', 'col'), 'row'), parts along dimension 2, may hold values from -6 to 6
- features: bfloat16 [2, 64, 32, 512], P(None, 'chan', ('groups', 'col'), 'row'), parts along dimension 2, may hold values from -6 to 6
- vol_target: bfloat16 [8, 40, 32, 512], P('chan', None, ('groups', 'col'), 'row'), parts along dimension 2, may hold values from -6 to 6
- offsets: int32 [4, 4], P('row', ('groups', 'col')), parts along dimension 1, may hold values from 0 to 2, as said below
- w_first: bfloat16 [64, 64, 3, 3], replicated, may hold values from -0.25 to 0.25
- w_second: bfloat16 [64, 64, 3, 3], replicated, may hold values from -0.25 to 0.25
Outputs:
- grad_features: bfloat16 [2, 64, 32, 512], P(None, 'chan', ('groups', 'col'), 'row'), parts along dimension 2
- grad_w_first: float32 [128, 64, 3, 3], P('groups'), parts along dimension 0
- grad_w_second: float32 [128, 64, 3, 3], P('groups'), parts along dimension 0
There are 2 independent parts, one for each index of `groups`. A program takes and returns all parts, laid end to end along the dimension named above; an argument that names none is the same for every part. Nothing has to cross between parts.
Inputs may be any that keep to these rules, and one draw needn't show every extreme that they name: `offsets`: each tile's entry is at most its own tile row index along the epipolar direction; tiles of the first row have 0, and some tile has exactly 2.
All inputs are finite; a program needn't handle non-finite values.
Results may differ from a plain program's by a relative error of at most 0.005.
Values may be sent and summed in bfloat16 or wider, within the bound.
A program may use at most 64 MiB of HBM per device.

v0:
```python
import math

import jax
import jax.numpy as jnp
from jax import lax
from jax.sharding import PartitionSpec as P

DISP = 40
MAXOFF = 2


def passed_along(block, axis, distance):
    devices = range(lax.axis_size(axis))
    route = [(i - distance, i) for i in devices if i - distance in devices]
    return lax.ppermute(block, axis, route)


def extended(array, sides, width):
    for axis, dim in sides:
        peers, length = (lax.axis_size(axis), array.shape[dim])
        up = [(i, (i + 1) % peers) for i in range(peers - 1)]
        down = [(j, i) for i, j in up]
        last = lax.slice_in_dim(array, length - width, length, axis=dim)
        leading = lax.slice_in_dim(array, 0, width, axis=dim)
        before = lax.ppermute(last, axis, up)
        after = lax.ppermute(leading, axis, down)
        array = jnp.concatenate([before, array, after], axis=dim)
    return array


def recompute_hidden(input_halo, w_first, tile_w, block_rows):
    summed = None
    for a in range(3):
        for b in range(3):
            product = jnp.einsum(
                "oi,nixy->noxy",
                w_first[:, :, a, b],
                input_halo[:, :, a : a + tile_w, b : b + block_rows],
                preferred_element_type=jnp.float32,
            )
            summed = product if summed is None else summed + product
    return jnp.maximum(summed, 0.0).astype(jnp.bfloat16)


def make_hidden(input_halo, w_first, tile_w, block_rows, first_ch, local_ch):
    hidden = recompute_hidden(input_halo, w_first, tile_w, block_rows)
    hidden_own = lax.dynamic_slice_in_dim(hidden, first_ch, local_ch, 1)
    return (hidden, hidden_own)


def correlate(left_feat, window, vol_target, block_rows):
    local_ch = left_feat.shape[0]
    tile_w = left_feat.shape[1]
    local_groups = vol_target.shape[0]
    group_size = local_ch // local_groups
    inv_size = 1.0 / group_size
    left_f32 = left_feat.astype(jnp.float32)

    def one_turn(t, state_now):
        left_grad, window_grad = state_now
        for j in range(8):
            d = t * 8 + j
            first_row = DISP - 1 - d
            window_rows = lax.dynamic_slice_in_dim(window, first_row, block_rows, 2).astype(
                jnp.float32
            )
            volume = (left_f32 * window_rows).reshape(
                local_groups, group_size, tile_w, block_rows
            ).sum(axis=1) * inv_size
            target_plane = lax.dynamic_index_in_dim(vol_target, d, 1, keepdims=False).astype(
                jnp.float32
            )
            weighted = jnp.repeat(volume - target_plane, group_size, axis=0) * inv_size
            left_grad = left_grad + weighted * window_rows
            window_part = (
                lax.dynamic_slice_in_dim(window_grad, first_row, block_rows, 2)
                + weighted * left_f32
            )
            window_grad = lax.dynamic_update_slice_in_dim(window_grad, window_part, first_row, 2)
        return (left_grad, window_grad)

    initial = (
        jnp.zeros((local_ch, tile_w, block_rows), jnp.float32),
        jnp.zeros((local_ch, tile_w, block_rows + DISP - 1), jnp.float32),
    )
    return lax.fori_loop(0, DISP // 8, one_turn, initial)


def body(layer_input, features, vol_target, offsets, w_first, w_second):
    all_channels = layer_input.shape[1]
    tile_w = layer_input.shape[2]
    block_rows = layer_input.shape[3]
    local_ch = features.shape[1]
    offset_here = offsets[0, 0]
    left_feat = features[0]
    right_feat = features[1]
    first_ch = lax.axis_index("chan") * local_ch
    main_rows = right_feat
    spill_rows = jnp.zeros((local_ch, tile_w, DISP - 1), jnp.bfloat16)
    for k in range(1, MAXOFF + 2):
        arrived = passed_along(right_feat, "row", k)
        main_rows = jnp.where(offset_here == k, arrived, main_rows)
        spill_rows = jnp.where(
            offset_here + 1 == k, arrived[:, :, block_rows - DISP + 1 :], spill_rows
        )
    window = jnp.concatenate([spill_rows, main_rows], axis=2)
    left_grad, window_grad = correlate(left_feat, window, vol_target, block_rows)
    main_grad = window_grad[:, :, DISP - 1 :]
    spill_grad = jnp.pad(
        window_grad[:, :, : DISP - 1], ((0, 0), (0, 0), (block_rows - DISP + 1, 0))
    )
    right_grad = jnp.where(offset_here == 0, main_grad, 0.0)
    for k in range(1, MAXOFF + 2):
        outgoing = jnp.where(offset_here == k, main_grad, 0.0) + jnp.where(
            offset_here + 1 == k, spill_grad, 0.0
        )
        right_grad = right_grad + passed_along(outgoing, "row", -k)
    grad_features = jnp.stack([left_grad, right_grad]).astype(jnp.bfloat16)
    grad_maps = lax.all_gather(grad_features, "chan", axis=1, tiled=True)
    joined = extended(
        jnp.concatenate([layer_input, grad_maps], axis=1), (("row", 3), ("col", 2)), 1
    )
    input_halo = joined[:, :all_channels]
    grad_halo = joined[:, all_channels:]
    hidden, hidden_here = make_hidden(input_halo, w_first, tile_w, block_rows, first_ch, local_ch)
    own_halo = lax.dynamic_slice_in_dim(grad_halo, first_ch, local_ch, 1)
    second_pieces = []
    for a in range(3):
        for b in range(3):
            view = own_halo[:, :, 2 - a : 2 - a + tile_w, 2 - b : 2 - b + block_rows]
            second_pieces.append(
                jnp.einsum("noxy,nixy->oi", view, hidden, preferred_element_type=jnp.float32)
            )
    second_local = jnp.stack(second_pieces, axis=-1).reshape(local_ch, all_channels, 3, 3)
    w2_cols = lax.dynamic_slice_in_dim(w_second, first_ch, local_ch, 1)
    summed = None
    for a in range(3):
        for b in range(3):
            view = grad_halo[:, :, 2 - a : 2 - a + tile_w, 2 - b : 2 - b + block_rows]
            product = jnp.einsum(
                "oi,noxy->nixy", w2_cols[:, :, a, b], view, preferred_element_type=jnp.float32
            )
            summed = product if summed is None else summed + product
    hidden_grad = jnp.where(hidden_here > 0, summed, 0.0).astype(jnp.bfloat16)
    first_pieces = []
    for a in range(3):
        for b in range(3):
            view = input_halo[:, :, a : a + tile_w, b : b + block_rows]
            first_pieces.append(
                jnp.einsum("noxy,nixy->oi", hidden_grad, view, preferred_element_type=jnp.float32)
            )
    first_local = jnp.stack(first_pieces, axis=-1).reshape(local_ch, all_channels, 3, 3)
    empty_grad = jnp.zeros((all_channels, all_channels, 3, 3), jnp.float32)
    first_full = lax.dynamic_update_slice_in_dim(empty_grad, first_local, first_ch, 0)
    second_full = lax.dynamic_update_slice_in_dim(empty_grad, second_local, first_ch, 0)
    first_sum, second_sum = lax.psum((first_full, second_full), ("row", "col", "chan"))
    factor = 1.0 / math.sqrt(
        2.0 * tile_w * lax.axis_size("col") * block_rows * lax.axis_size("row")
    )
    return (grad_features, first_sum * factor, second_sum * factor)


def solution(mesh):
    return jax.shard_map(
        body,
        mesh=mesh,
        in_specs=(
            P(None, None, ("groups", "col"), "row"),
            P(None, "chan", ("groups", "col"), "row"),
            P("chan", None, ("groups", "col"), "row"),
            P("row", ("groups", "col")),
            P(),
            P(),
        ),
        out_specs=(
            P(None, "chan", ("groups", "col"), "row"),
            P("groups", None, None, None),
            P("groups", None, None, None),
        ),
        check_vma=False,
    )
```

profile of v0, /device:TPU:1, one launch (start us, length us, event | category | flops | bytes accessed | tf_op | source)
XLA Modules:
  0.0 373.3 jit_solution(15215072760396662357)
XLA Ops:
  8.2 6.1 %collective-permute-start = (bf16[32,8,128]{2,0,1:T(8,128)(2,1)S(1)}, bf16[32,8,128]{2,0,1:T(8,128)(2,1)S(1)}, u32[]{:S(2)}, u32[]{:S(2)}) collective-permute-start(bf16[32,8,128]{2,0,1:T(8,128)(2,1)S(1)} %bitcast.440), channel_id=1, source_target_pairs={{0,12},{1,13},{2,14},{3,15},{16,28},{17,29},{18,30},{19,31}} | collective-permute-start | bytes 196616 | tf_op jit(solution)/shard_map/ppermute | solution.py:15
  20.1 197.9 %while.19 = (s32[]{:T(128)}, f32[32,8,128]{2,1,0:T(8,128)S(1)}, f32[32,8,167]{2,1,0:T(8,128)S(1)}, bf16[32,8,167]{2,1,0:T(8,128)(2,1)S(1)}, f32[32,8,128]{2,1,0:...) while((s32[]{:T(128)}, f32[32,8,128]{2,1,0:T(8,128)S(1)}, ...), condition=%wide.region_9.10_spmd.clone, body=%wide.region_0.9_spmd.clone.sunk | while | flops 2228291 | bytes 7406695 | solution.py:86
  20.8 4.8 %dynamic_update_slice.114 = f32[32,8,167]{2,1,0:T(8,128)S(1)} dynamic-update-slice(f32[32,8,167]{2,1,0:T(8,128)S(1)} %get-tuple-element.376, f32[32,8,128]{2,1,0:T(8,128)S(1)} %fusion.177, s32[]{:T(128)} %constant.221.clone.1..sunk, s32[]{:T(128)} %constant.221.clone.1..sunk, s32[]{:T(128)S(6)} %select_n.377) | dynamic-update-slice | bytes 262148 | tf_op jit(solution)/shard_map/while/body/eval_jaxpr/dynamic_update_slice | solution.py:79
  25.7 4.8 %dynamic_update_slice.115 = f32[32,8,167]{2,1,0:T(8,128)S(1)} dynamic-update-slice(f32[32,8,167]{2,1,0:T(8,128)S(1)} %dynamic_update_slice.114, f32[32,8,128]{2,1,0:T(8,128)S(1)} %fusion.178, s32[]{:T(128)} %constant.221.clone.1..sunk, s32[]{:T(128)} %constant.221.clone.1..sunk, s32[]{:T(128)S(6)} %select_n.384) | dynamic-update-slice | bytes 262148 | tf_op jit(solution)/shard_map/while/body/eval_jaxpr/dynamic_update_slice | solution.py:79
  30.7 4.8 %dynamic_update_slice.116 = f32[32,8,167]{2,1,0:T(8,128)S(1)} dynamic-update-slice(f32[32,8,167]{2,1,0:T(8,128)S(1)} %dynamic_update_slice.115, f32[32,8,128]{2,1,0:T(8,128)S(1)} %fusion.179, s32[]{:T(128)} %constant.221.clone.1..sunk, s32[]{:T(128)} %constant.221.clone.1..sunk, s32[]{:T(128)S(6)} %select_n.383) | dynamic-update-slice | bytes 262148 | tf_op jit(solution)/shard_map/while/body/eval_jaxpr/dynamic_update_slice | solution.py:79
  35.6 4.8 %dynamic_update_slice.117 = f32[32,8,167]{2,1,0:T(8,128)S(1)} dynamic-update-slice(f32[32,8,167]{2,1,0:T(8,128)S(1)} %dynamic_update_slice.116, f32[32,8,128]{2,1,0:T(8,128)S(1)} %fusion.180, s32[]{:T(128)} %constant.221.clone.1..sunk, s32[]{:T(128)} %constant.221.clone.1..sunk, s32[]{:T(128)S(6)} %select_n.382) | dynamic-update-slice | bytes 262148 | tf_op jit(solution)/shard_map/while/body/eval_jaxpr/dynamic_update_slice | solution.py:79
  40.6 4.8 %dynamic_update_slice.118 = f32[32,8,167]{2,1,0:T(8,128)S(1)} dynamic-update-slice(f32[32,8,167]{2,1,0:T(8,128)S(1)} %dynamic_update_slice.117, f32[32,8,128]{2,1,0:T(8,128)S(1)} %fusion.181, s32[]{:T(128)} %constant.221.clone.1..sunk, s32[]{:T(128)} %constant.221.clone.1..sunk, s32[]{:T(128)S(6)} %select_n.381) | dynamic-update-slice | bytes 262148 | tf_op jit(solution)/shard_map/while/body/eval_jaxpr/dynamic_update_slice | solution.py:79
  45.5 4.8 %dynamic_update_slice.119 = f32[32,8,167]{2,1,0:T(8,128)S(1)} dynamic-update-slice(f32[32,8,167]{2,1,0:T(8,128)S(1)} %dynamic_update_slice.118, f32[32,8,128]{2,1,0:T(8,128)S(1)} %fusion.182, s32[]{:T(128)} %constant.221.clone.1..sunk, s32[]{:T(128)} %constant.221.clone.1..sunk, s32[]{:T(128)S(6)} %select_n.380) | dynamic-update-slice | bytes 262148 | tf_op jit(solution)/shard_map/while/body/eval_jaxpr/dynamic_update_slice | solution.py:79
  50.5 4.8 %dynamic_update_slice.120 = f32[32,8,167]{2,1,0:T(8,128)S(1)} dynamic-update-slice(f32[32,8,167]{2,1,0:T(8,128)S(1)} %dynamic_update_slice.119, f32[32,8,128]{2,1,0:T(8,128)S(1)} %fusion.183, s32[]{:T(128)} %constant.221.clone.1..sunk, s32[]{:T(128)} %constant.221.clone.1..sunk, s32[]{:T(128)S(6)} %select_n.379) | dynamic-update-slice | bytes 262148 | tf_op jit(solution)/shard_map/while/body/eval_jaxpr/dynamic_update_slice | solution.py:79
  55.4 4.8 %dynamic_update_slice.121 = f32[32,8,167]{2,1,0:T(8,128)S(1)} dynamic-update-slice(f32[32,8,167]{2,1,0:T(8,128)S(1)} %dynamic_update_slice.120, f32[32,8,128]{2,1,0:T(8,128)S(1)} %fusion.184, s32[]{:T(128)} %constant.221.clone.1..sunk, s32[]{:T(128)} %constant.221.clone.1..sunk, s32[]{:T(128)S(6)} %select_n.378) | dynamic-update-slice | bytes 262148 | tf_op jit(solution)/shard_map/while/body/eval_jaxpr/dynamic_update_slice | solution.py:79
  61.2 4.8 %dynamic_update_slice.114 = f32[32,8,167]{2,1,0:T(8,128)S(1)} dynamic-update-slice(f32[32,8,167]{2,1,0:T(8,128)S(1)} %get-tuple-element.376, f32[32,8,128]{2,1,0:T(8,128)S(1)} %fusion.177, s32[]{:T(128)} %constant.221.clone.1..sunk, s32[]{:T(128)} %constant.221.clone.1..sunk, s32[]{:T(128)S(6)} %select_n.377) | dynamic-update-slice | bytes 262148 | tf_op jit(solution)/shard_map/while/body/eval_jaxpr/dynamic_update_slice | solution.py:79
  66.2 4.8 %dynamic_update_slice.115 = f32[32,8,167]{2,1,0:T(8,128)S(1)} dynamic-update-slice(f32[32,8,167]{2,1,0:T(8,128)S(1)} %dynamic_update_slice.114, f32[32,8,128]{2,1,0:T(8,128)S(1)} %fusion.178, s32[]{:T(128)} %constant.221.clone.1..sunk, s32[]{:T(128)} %constant.221.clone.1..sunk, s32[]{:T(128)S(6)} %select_n.384) | dynamic-update-slice | bytes 262148 | tf_op jit(solution)/shard_map/while/body/eval_jaxpr/dynamic_update_slice | solution.py:79
  71.1 4.8 %dynamic_update_slice.116 = f32[32,8,167]{2,1,0:T(8,128)S(1)} dynamic-update-slice(f32[32,8,167]{2,1,0:T(8,128)S(1)} %dynamic_update_slice.115, f32[32,8,128]{2,1,0:T(8,128)S(1)} %fusion.179, s32[]{:T(128)} %constant.221.clone.1..sunk, s32[]{:T(128)} %constant.221.clone.1..sunk, s32[]{:T(128)S(6)} %select_n.383) | dynamic-update-slice | bytes 262148 | tf_op jit(solution)/shard_map/while/body/eval_jaxpr/dynamic_update_slice | solution.py:79
  76.1 4.8 %dynamic_update_slice.117 = f32[32,8,167]{2,1,0:T(8,128)S(1)} dynamic-update-slice(f32[32,8,167]{2,1,0:T(8,128)S(1)} %dynamic_update_slice.116, f32[32,8,128]{2,1,0:T(8,128)S(1)} %fusion.180, s32[]{:T(128)} %constant.221.clone.1..sunk, s32[]{:T(128)} %constant.221.clone.1..sunk, s32[]{:T(128)S(6)} %select_n.382) | dynamic-update-slice | bytes 262148 | tf_op jit(solution)/shard_map/while/body/eval_jaxpr/dynamic_update_slice | solution.py:79
  81.0 4.8 %dynamic_update_slice.118 = f32[32,8,167]{2,1,0:T(8,128)S(1)} dynamic-update-slice(f32[32,8,167]{2,1,0:T(8,128)S(1)} %dynamic_update_slice.117, f32[32,8,128]{2,1,0:T(8,128)S(1)} %fusion.181, s32[]{:T(128)} %constant.221.clone.1..sunk, s32[]{:T(128)} %constant.221.clone.1..sunk, s32[]{:T(128)S(6)} %select_n.381) | dynamic-update-slice | bytes 262148 | tf_op jit(solution)/shard_map/while/body/eval_jaxpr/dynamic_update_slice | solution.py:79
  86.0 4.8 %dynamic_update_slice.119 = f32[32,8,167]{2,1,0:T(8,128)S(1)} dynamic-update-slice(f32[32,8,167]{2,1,0:T(8,128)S(1)} %dynamic_update_slice.118, f32[32,8,128]{2,1,0:T(8,128)S(1)} %fusion.182, s32[]{:T(128)} %constant.221.clone.1..sunk, s32[]{:T(128)} %constant.221.clone.1..sunk, s32[]{:T(128)S(6)} %select_n.380) | dynamic-update-slice | bytes 262148 | tf_op jit(solution)/shard_map/while/body/eval_jaxpr/dynamic_update_slice | solution.py:79
  90.9 4.8 %dynamic_update_slice.120 = f32[32,8,167]{2,1,0:T(8,128)S(1)} dynamic-update-slice(f32[32,8,167]{2,1,0:T(8,128)S(1)} %dynamic_update_slice.119, f32[32,8,128]{2,1,0:T(8,128)S(1)} %fusion.183, s32[]{:T(128)} %constant.221.clone.1..sunk, s32[]{:T(128)} %constant.221.clone.1..sunk, s32[]{:T(128)S(6)} %select_n.379) | dynamic-update-slice | bytes 262148 | tf_op jit(solution)/shard_map/while/body/eval_jaxpr/dynamic_update_slice | solution.py:79
  95.9 4.8 %dynamic_update_slice.121 = f32[32,8,167]{2,1,0:T(8,128)S(1)} dynamic-update-slice(f32[32,8,167]{2,1,0:T(8,128)S(1)} %dynamic_update_slice.120, f32[32,8,128]{2,1,0:T(8,128)S(1)} %fusion.184, s32[]{:T(128)} %constant.221.clone.1..sunk, s32[]{:T(128)} %constant.221.clone.1..sunk, s32[]{:T(128)S(6)} %select_n.378) | dynamic-update-slice | bytes 262148 | tf_op jit(solution)/shard_map/while/body/eval_jaxpr/dynamic_update_slice | solution.py:79
  101.6 4.8 %dynamic_update_slice.114 = f32[32,8,167]{2,1,0:T(8,128)S(1)} dynamic-update-slice(f32[32,8,167]{2,1,0:T(8,128)S(1)} %get-tuple-element.376, f32[32,8,128]{2,1,0:T(8,128)S(1)} %fusion.177, s32[]{:T(128)} %constant.221.clone.1..sunk, s32[]{:T(128)} %constant.221.clone.1..sunk, s32[]{:T(128)S(6)} %select_n.377) | dynamic-update-slice | bytes 262148 | tf_op jit(solution)/shard_map/while/body/eval_jaxpr/dynamic_update_slice | solution.py:79
  106.6 4.8 %dynamic_update_slice.115 = f32[32,8,167]{2,1,0:T(8,128)S(1)} dynamic-update-slice(f32[32,8,167]{2,1,0:T(8,128)S(1)} %dynamic_update_slice.114, f32[32,8,128]{2,1,0:T(8,128)S(1)} %fusion.178, s32[]{:T(128)} %constant.221.clone.1..sunk, s32[]{:T(128)} %constant.221.clone.1..sunk, s32[]{:T(128)S(6)} %select_n.384) | dynamic-update-slice | bytes 262148 | tf_op jit(solution)/shard_map/while/body/eval_jaxpr/dynamic_update_slice | solution.py:79
  111.6 4.8 %dynamic_update_slice.116 = f32[32,8,167]{2,1,0:T(8,128)S(1)} dynamic-update-slice(f32[32,8,167]{2,1,0:T(8,128)S(1)} %dynamic_update_slice.115, f32[32,8,128]{2,1,0:T(8,128)S(1)} %fusion.179, s32[]{:T(128)} %constant.221.clone.1..sunk, s32[]{:T(128)} %constant.221.clone.1..sunk, s32[]{:T(128)S(6)} %select_n.383) | dynamic-update-slice | bytes 262148 | tf_op jit(solution)/shard_map/while/body/eval_jaxpr/dynamic_update_slice | solution.py:79
  116.5 4.8 %dynamic_update_slice.117 = f32[32,8,167]{2,1,0:T(8,128)S(1)} dynamic-update-slice(f32[32,8,167]{2,1,0:T(8,128)S(1)} %dynamic_update_slice.116, f32[32,8,128]{2,1,0:T(8,128)S(1)} %fusion.180, s32[]{:T(128)} %constant.221.clone.1..sunk, s32[]{:T(128)} %constant.221.clone.1..sunk, s32[]{:T(128)S(6)} %select_n.382) | dynamic-update-slice | bytes 262148 | tf_op jit(solution)/shard_map/while/body/eval_jaxpr/dynamic_update_slice | solution.py:79
  121.5 4.8 %dynamic_update_slice.118 = f32[32,8,167]{2,1,0:T(8,128)S(1)} dynamic-update-slice(f32[32,8,167]{2,1,0:T(8,128)S(1)} %dynamic_update_slice.117, f32[32,8,128]{2,1,0:T(8,128)S(1)} %fusion.181, s32[]{:T(128)} %constant.221.clone.1..sunk, s32[]{:T(128)} %constant.221.clone.1..sunk, s32[]{:T(128)S(6)} %select_n.381) | dynamic-update-slice | bytes 262148 | tf_op jit(solution)/shard_map/while/body/eval_jaxpr/dynamic_update_slice | solution.py:79
  136.3 4.8 %dynamic_update_slice.121 = f32[32,8,167]{2,1,0:T(8,128)S(1)} dynamic-update-slice(f32[32,8,167]{2,1,0:T(8,128)S(1)} %dynamic_update_slice.120, f32[32,8,128]{2,1,0:T(8,128)S(1)} %fusion.184, s32[]{:T(128)} %constant.221.clone.1..sunk, s32[]{:T(128)} %constant.221.clone.1..sunk, s32[]{:T(128)S(6)} %select_n.378) | dynamic-update-slice | bytes 262148 | tf_op jit(solution)/shard_map/while/body/eval_jaxpr/dynamic_update_slice | solution.py:79
  166.9 4.8 %dynamic_update_slice.119 = f32[32,8,167]{2,1,0:T(8,128)S(1)} dynamic-update-slice(f32[32,8,167]{2,1,0:T(8,128)S(1)} %dynamic_update_slice.118, f32[32,8,128]{2,1,0:T(8,128)S(1)} %fusion.182, s32[]{:T(128)} %constant.221.clone.1..sunk, s32[]{:T(128)} %constant.221.clone.1..sunk, s32[]{:T(128)S(6)} %select_n.380) | dynamic-update-slice | bytes 262148 | tf_op jit(solution)/shard_map/while/body/eval_jaxpr/dynamic_update_slice | solution.py:79
  171.8 4.8 %dynamic_update_slice.120 = f32[32,8,167]{2,1,0:T(8,128)S(1)} dynamic-update-slice(f32[32,8,167]{2,1,0:T(8,128)S(1)} %dynamic_update_slice.119, f32[32,8,128]{2,1,0:T(8,128)S(1)} %fusion.183, s32[]{:T(128)} %constant.221.clone.1..sunk, s32[]{:T(128)} %constant.221.clone.1..sunk, s32[]{:T(128)S(6)} %select_n.379) | dynamic-update-slice | bytes 262148 | tf_op jit(solution)/shard_map/while/body/eval_jaxpr/dynamic_update_slice | solution.py:79
  197.4 4.8 %dynamic_update_slice.117 = f32[32,8,167]{2,1,0:T(8,128)S(1)} dynamic-update-slice(f32[32,8,167]{2,1,0:T(8,128)S(1)} %dynamic_update_slice.116, f32[32,8,128]{2,1,0:T(8,128)S(1)} %fusion.180, s32[]{:T(128)} %constant.221.clone.1..sunk, s32[]{:T(128)} %constant.221.clone.1..sunk, s32[]{:T(128)S(6)} %select_n.382) | dynamic-update-slice | bytes 262148 | tf_op jit(solution)/shard_map/while/body/eval_jaxpr/dynamic_update_slice | solution.py:79
  202.3 4.8 %dynamic_update_slice.118 = f32[32,8,167]{2,1,0:T(8,128)S(1)} dynamic-update-slice(f32[32,8,167]{2,1,0:T(8,128)S(1)} %dynamic_update_slice.117, f32[32,8,128]{2,1,0:T(8,128)S(1)} %fusion.181, s32[]{:T(128)} %constant.221.clone.1..sunk, s32[]{:T(128)} %constant.221.clone.1..sunk, s32[]{:T(128)S(6)} %select_n.381) | dynamic-update-slice | bytes 262148 | tf_op jit(solution)/shard_map/while/body/eval_jaxpr/dynamic_update_slice | solution.py:79
  224.0 5.7 %collective-permute-done.4 = f32[32,8,128]{2,0,1:T(8,128)S(1)} collective-permute-done((f32[32,8,128]{2,0,1:T(8,128)S(1)}, f32[32,8,128]{2,0,1:T(8,128)S(1)}, u32[]{:S(2)}, u32[]{:S(2)}) %collective-permute-start.4) | collective-permute-done | bytes 131104 | tf_op jit(solution)/shard_map/ppermute | solution.py:15
  233.2 5.0 %all_gather.3 = bf16[2,64,8,128]{3,1,2,0:T(8,128)(2,1)S(1)} all-gather(bf16[2,32,8,128]{3,1,2,0:T(8,128)(2,1)S(1)} %pad_maximum_fusion.11), channel_id=1, replica_groups=mesh['groups'=2,'row'=4,'col'=2,'chan'=2] {'chan'}, dimensions={1}, use_global_device_ids=true | all-gather | bytes 393216 | tf_op jit(solution)/shard_map/all_gather | solution.py:119
  241.4 9.6 %collective-permute-done.6 = bf16[2,128,8,1]{3,1,2,0:T(8,128)(2,1)S(1)} collective-permute-done((bf16[2,128,8,1]{3,1,2,0:T(8,128)(2,1)S(1)}, bf16[2,128,8,1]{3,1,2,0:T(8,128)(2,1)S(1)}, u32[]{:S(2)}, u32[]{:S(2)}) %collective-permute-start.6) | collective-permute-done | bytes 4128 | tf_op jit(solution)/shard_map/ppermute | solution.py:25
  275.2 89.4 %all-reduce.4.cloned.1.call-done = (f32[64,64,3,3]{1,0,3,2:T(8,128)}, f32[64,64,3,3]{1,0,3,2:T(8,128)}) async-done(((f32[64,64,3,3]{1,0,3,2:T(8,128)}, f32[64,64,3,3]{1,0,3,2:T(8,128)}), (f32[64,64,3,3]{1,0,3,2:T(8,128)}, f32[64,64,3,3]{1,0,3,2:T(8,128)})) %all-reduce.4.cloned.1.call-update) | async-done | bytes 294928 | tf_op jit(solution)/shard_map/psum | solution.py:156
  (164 shorter events, 115.4 us)
Async XLA Ops:
  7.2 233.9 %copy-start = (bf16[64,64,3,3]{1,0,3,2:T(8,128)(2,1)S(1)}, bf16[64,64,3,3]{1,0,3,2:T(8,128)(2,1)}, u32[]{:S(2)}) copy-start(bf16[64,64,3,3]{1,0,3,2:T(8,128)(2,1)} %param.13) | copy-start | bytes 221188
  7.2 12.5 %copy-start.4 = (bf16[4,40,8,128]{3,2,1,0:T(8,128)(2,1)S(1)}, bf16[4,40,8,128]{3,2,1,0:T(8,128)(2,1)}, u32[]{:S(2)}) copy-start(bf16[4,40,8,128]{3,2,1,0:T(8,128)(2,1)} %param.10) | copy-start | bytes 983044
  7.2 357.4 %all-reduce.4.cloned.1.call-start = ((), (), s32[]{:S(2)}) async-start(), calls=%async_computation | async-start | bytes 1179648 | tf_op jit(solution)/shard_map/psum | solution.py:156
  8.2 11.5 %collective-permute-start = (bf16[32,8,128]{2,0,1:T(8,128)(2,1)S(1)}, bf16[32,8,128]{2,0,1:T(8,128)(2,1)S(1)}, u32[]{:S(2)}, u32[]{:S(2)}) collective-permute-start(bf16[32,8,128]{2,0,1:T(8,128)(2,1)S(1)} %bitcast.440), channel_id=1, source_target_pairs={{0,12},{1,13},{2,14},{3,15},{16,28},{17,29},{18,30},{19,31}} | collective-permute-start | bytes 196616 | tf_op jit(solution)/shard_map/ppermute | solution.py:15
  14.3 5.5 %collective-permute-start.1 = (bf16[32,8,128]{2,0,1:T(8,128)(2,1)S(1)}, bf16[32,8,128]{2,0,1:T(8,128)(2,1)S(1)}, u32[]{:S(2)}, u32[]{:S(2)}) collective-permute-start(bf16[32,8,128]{2,0,1:T(8,128)(2,1)S(1)} %bitcast.441), channel_id=1, source_target_pairs={{0,8},{4,12},{1,9},{5,13},{2,10},{6,14},{3,11},{7,15},{16,24},{20,... | collective-permute-start | bytes 196616 | tf_op jit(solution)/shard_map/ppermute | solution.py:15
  15.6 4.2 %collective-permute-start.2 = (bf16[32,8,128]{2,0,1:T(8,128)(2,1)S(1)}, bf16[32,8,128]{2,0,1:T(8,128)(2,1)S(1)}, u32[]{:S(2)}, u32[]{:S(2)}) collective-permute-start(bf16[32,8,128]{2,0,1:T(8,128)(2,1)S(1)} %bitcast.442), channel_id=1, source_target_pairs={{0,4},{4,8},{8,12},{1,5},{5,9},{9,13},{2,6},{6,10},{10,14},{3,7},{... | collective-permute-start | bytes 196616 | tf_op jit(solution)/shard_map/ppermute | solution.py:15
  218.0 4.2 %copy-start.1 = (bf16[2,64,8,128]{3,2,1,0:T(8,128)(2,1)S(1)}, bf16[2,64,8,128]{3,2,1,0:T(8,128)(2,1)}, u32[]{:S(2)}) copy-start(bf16[2,64,8,128]{3,2,1,0:T(8,128)(2,1)} %param.8) | copy-start | bytes 786436
  218.3 5.7 %collective-permute-start.3 = (f32[32,8,128]{2,0,1:T(8,128)S(1)}, f32[32,8,128]{2,0,1:T(8,128)S(1)}, u32[]{:S(2)}, u32[]{:S(2)}) collective-permute-start(f32[32,8,128]{2,0,1:T(8,128)S(1)} %get-tuple-element.273), channel_id=1, source_target_pairs={{4,0},{8,4},{12,8},{5,1},{9,5},{13,9},{6,2},{10,6},{14,10},{7,3},{... | collective-permute-start | bytes 393224 | tf_op jit(solution)/shard_map/ppermute | solution.py:15
  219.6 10.1 %collective-permute-start.4 = (f32[32,8,128]{2,0,1:T(8,128)S(1)}, f32[32,8,128]{2,0,1:T(8,128)S(1)}, u32[]{:S(2)}, u32[]{:S(2)}) collective-permute-start(f32[32,8,128]{2,0,1:T(8,128)S(1)} %get-tuple-element.274), channel_id=1, source_target_pairs={{8,0},{12,4},{9,1},{13,5},{10,2},{14,6},{11,3},{15,7},{24,16},{28,... | collective-permute-start | bytes 393224 | tf_op jit(solution)/shard_map/ppermute | solution.py:15
  220.9 12.1 %collective-permute-start.5 = (f32[32,8,128]{2,0,1:T(8,128)S(1)}, f32[32,8,128]{2,0,1:T(8,128)S(1)}, u32[]{:S(2)}, u32[]{:S(2)}) collective-permute-start(f32[32,8,128]{2,0,1:T(8,128)S(1)} %get-tuple-element.275), channel_id=1, source_target_pairs={{12,0},{13,1},{14,2},{15,3},{28,16},{29,17},{30,18},{31,19}} | collective-permute-start | bytes 393224 | tf_op jit(solution)/shard_map/ppermute | solution.py:15
  238.4 12.5 %collective-permute-start.6 = (bf16[2,128,8,1]{3,1,2,0:T(8,128)(2,1)S(1)}, bf16[2,128,8,1]{3,1,2,0:T(8,128)(2,1)S(1)}, u32[]{:S(2)}, u32[]{:S(2)}) collective-permute-start(bf16[2,128,8,1]{3,1,2,0:T(8,128)(2,1)S(1)} %get-tuple-element.271), channel_id=1, source_target_pairs={{0,4},{4,8},{8,12},{1,5},{5,9},{9,13},{2,6},{6,10},{10,14},{3,7},{... | collective-permute-start | bytes 12296 | tf_op jit(solution)/shard_map/ppermute | solution.py:25
  239.8 15.0 %collective-permute-start.7 = (bf16[2,128,8,1]{3,1,2,0:T(8,128)(2,1)S(1)}, bf16[2,128,8,1]{3,1,2,0:T(8,128)(2,1)S(1)}, u32[]{:S(2)}, u32[]{:S(2)}) collective-permute-start(bf16[2,128,8,1]{3,1,2,0:T(8,128)(2,1)S(1)} %get-tuple-element.272), channel_id=1, source_target_pairs={{4,0},{8,4},{12,8},{5,1},{9,5},{13,9},{6,2},{10,6},{14,10},{7,3},{... | collective-permute-start | bytes 12296 | tf_op jit(solution)/shard_map/ppermute | solution.py:26
  255.0 5.1 %copy-start.5 = (bf16[64,64,3,3]{1,0,3,2:T(8,128)(2,1)S(1)}, bf16[64,64,3,3]{1,0,3,2:T(8,128)(2,1)}, u32[]{:S(2)}) copy-start(bf16[64,64,3,3]{1,0,3,2:T(8,128)(2,1)} %param.12) | copy-start | bytes 221188
  255.0 5.7 %collective-permute-start.8 = (bf16[2,128,1,130]{3,1,2,0:T(8,128)(2,1)S(1)}, bf16[2,128,1,130]{3,1,2,0:T(8,128)(2,1)S(1)}, u32[]{:S(2)}, u32[]{:S(2)}) collective-permute-start(bf16[2,128,1,130]{3,1,2,0:T(8,128)(2,1)S(1)} %get-tuple-element.267), channel_id=1, source_target_pairs={{0,2},{1,3},{4,6},{5,7},{8,10},{9,11},{12,14},{13,15},{16,18},{17,... | collective-permute-start | bytes 199688 | tf_op jit(solution)/shard_map/ppermute | solution.py:25
  258.3 5.7 %collective-permute-start.9 = (bf16[2,128,1,130]{3,1,2,0:T(8,128)(2,1)S(1)}, bf16[2,128,1,130]{3,1,2,0:T(8,128)(2,1)S(1)}, u32[]{:S(2)}, u32[]{:S(2)}) collective-permute-start(bf16[2,128,1,130]{3,1,2,0:T(8,128)(2,1)S(1)} %get-tuple-element.268), channel_id=1, source_target_pairs={{2,0},{3,1},{6,4},{7,5},{10,8},{11,9},{14,12},{15,13},{18,16},{19,... | collective-permute-start | bytes 199688 | tf_op jit(solution)/shard_map/ppermute | solution.py:26
  273.6 0.7 copy-start.3
  273.7 0.7 copy-start.2
Sparse Core Ops, SparseCore 0:
  274.6 89.9 all-reduce.3
where the time goes:
time: 375 us; the launch traced here: 373 us
  local copies, waits for them, and re-layouts  191 us (51%)
  waiting for transfers between devices  117 us (31%)
  starting transfers between devices  20.8 us (6%)
  between operations  15.2 us (4%)
  other arithmetic  12.7 us (3%)
  matrix products  10.3 us (3%)
  blocking collectives  4.97 us (1%)
    dynamic_update_slice x40, local copies, waits for them, and re-layouts, one_turn(): lax.dynamic_update_slice_in_dim(window_grad, window_part, first_row, 2)  189 us
    psum x1, waiting for transfers between devices, body(): lax.psum((first_full, second_full), ('row', 'col', 'chan'))  89.4 us
    ppermute x6, starting transfers between devices, passed_along(): return lax.ppermute(block, axis, route)  13.4 us
    ppermute x6, waiting for transfers between devices, passed_along(): return lax.ppermute(block, axis, route)  10.7 us
    ppermute x2, waiting for transfers between devices, extended(): before = lax.ppermute(last, axis, up)  9.62 us
  transfers between devices with their start and end apart: 11, of which 7 were waited for; matrix products, arithmetic and copies ran while one was open for 1% of the time, Pallas kernels for 0%

commit v1 on v0

v1 whole, which is shorter than its diff:
```python
import functools
import math

import jax
import jax.numpy as jnp
from jax import lax
from jax.experimental import pallas as pl
from jax.experimental.pallas import tpu as pltpu
from jax.sharding import PartitionSpec as P

MAXOFF = 2
REACH = MAXOFF + 1
MESH = pl.DeviceIdType.MESH
SIDES = [(dr, dc) for dr in (-1, 1) for dc in (-1, 0, 1)]
F32 = jnp.float32
BF16 = jnp.bfloat16


def vmem():
    return pl.BlockSpec(memory_space=pltpu.VMEM)


class Place:
    def __init__(self, sizes):
        self.sizes = sizes
        self.at = {axis: lax.axis_index(axis) for axis in sizes}

    def step(self, **moves):
        return {
            axis: lax.rem(self.at[axis] + (move + self.sizes[axis]), self.sizes[axis])
            for axis, move in moves.items()
        }


def greet(place, moves):
    barrier = pltpu.get_barrier_semaphore()
    for move in moves:
        back = {axis: -by for axis, by in move.items()}
        pl.semaphore_signal(barrier, inc=1, device_id=place.step(**back), device_id_type=MESH)
    pl.semaphore_wait(barrier, len(moves))


def send(place, move, src, dst, send_sem, recv_sem, at):
    copy = pltpu.make_async_remote_copy(
        src_ref=src,
        dst_ref=dst,
        send_sem=send_sem.at[at],
        recv_sem=recv_sem.at[at],
        device_id=place.step(**move),
        device_id_type=MESH,
    )
    copy.start()
    return copy


def packed_edges(tile_of, images, tile_w, lanes):
    width = lanes.shape[1]
    count = images * tile_w
    packed = jnp.zeros(lanes.shape, F32)
    for k in range(count):
        tile = tile_of(k // tile_w, k % tile_w)
        packed = jnp.where(lanes == k, pltpu.roll(tile, k + 1, 1), packed)
        packed = jnp.where(lanes == count + k, pltpu.roll(tile, count + k, 1), packed)
    return packed


def rolled(value, by):
    by = by % value.shape[-1]
    return value if by == 0 else pltpu.roll(value, by, value.ndim - 1)


def fill_views(views, place, tile_of, side_of, edges_of, images, tile_w, lanes):
    width = lanes.shape[1]
    count = images * tile_w
    row, col = place.at["row"], place.at["col"]
    rows, cols = place.sizes["row"], place.sizes["col"]
    inside_row = {-1: (row > 0).astype(F32), 1: (row < rows - 1).astype(F32)}
    inside_col = {-1: (col > 0).astype(F32), 0: 1.0, 1: (col < cols - 1).astype(F32)}
    for dc in (-1, 0, 1):
        before = edges_of(SIDES.index((-1, dc))) * (inside_row[-1] * inside_col[dc])
        after = edges_of(SIDES.index((1, dc))) * (inside_row[1] * inside_col[dc])
        places = {-1: [0], 0: range(1, tile_w + 1), 1: [tile_w + 1]}[dc]
        for n in range(images):
            for xx in places:
                if dc == 0:
                    tile = tile_of(n, xx - 1)
                    k = n * tile_w + xx - 1
                else:
                    tile = side_of(0 if dc < 0 else 1, n) * inside_col[dc]
                    k = n * tile_w + (tile_w - 1 if dc < 0 else 0)
                left = jnp.where(lanes == 0, rolled(before, -k), rolled(tile, 1))
                right = jnp.where(
                    lanes == width - 1, rolled(after, width - 1 - count - k), rolled(tile, -1)
                )
                views[n, xx, 0] = left.astype(BF16)
                views[n, xx, 1] = tile.astype(BF16)
                views[n, xx, 2] = right.astype(BF16)


def lane_index(shape):
    return lax.broadcasted_iota(jnp.int32, shape, len(shape) - 1)


def fetch_kernel(sizes, right_ref, image_ref, window_ref, edges_ref, side_ref, pack, send_sem, recv_sem):
    place = Place(sizes)
    images, tile_w, channels, width = image_ref.shape
    moves = [{"row": k} for k in range(1, REACH + 1)]
    moves += [{"col": 1}, {"col": -1}]
    moves += [{"row": -dr, "col": -dc} for dr, dc in SIDES]
    greet(place, moves)
    copies = []
    for k in range(REACH):
        copies.append(send(place, moves[k], right_ref, window_ref.at[k], send_sem, recv_sem, k))
    for side, x in ((0, tile_w - 1), (1, 0)):
        at = REACH + side
        copies.append(
            send(place, moves[at], image_ref.at[:, x], side_ref.at[side], send_sem, recv_sem, at)
        )
    lanes = lane_index((channels, width))
    pack[...] = packed_edges(
        lambda n, x: image_ref[n, x].astype(F32), images, tile_w, lanes
    ).astype(BF16)
    for j in range(len(SIDES)):
        at = REACH + 2 + j
        copies.append(send(place, moves[at], pack, edges_ref.at[j], send_sem, recv_sem, at))
    for copy in copies:
        copy.wait()


def correlate_kernel(
    sizes, offset_ref, left_ref, right_ref, window_ref, target_ref, image_ref, edges_ref, side_ref,
    w_ref, left_grad_ref, own_ref, out_ref, hidden_ref, views_ref, main_s, spill_s,
):
    place = Place(sizes)
    images, tile_w, channels, width = image_ref.shape
    groups, disp = target_ref.shape[:2]
    size = left_ref.shape[0] // groups
    inv = 1.0 / size
    offset = offset_ref[0, 0]
    row = place.at["row"]
    lanes = lane_index((tile_w, width))
    spill_in = [jnp.logical_and(offset + 1 == k, row >= k).astype(F32) for k in range(1, REACH + 1)]
    main_in = [(offset == k).astype(F32) for k in range(REACH)]

    def one_group(g, carry):
        first = pl.multiple_of(g * size, size)
        chans = pl.ds(first, size)
        got = [right_ref[chans].astype(F32)]
        got += [window_ref[k, chans].astype(F32) for k in range(REACH)]
        main_s[...] = sum(got[k] * main_in[k] for k in range(REACH))
        spill_s[...] = sum(got[k + 1] * spill_in[k] for k in range(REACH))

        def step(t, state):
            left_grad, main_grad, spill_grad = state
            left = left_ref[chans].astype(F32)
            for j in range(8):
                d = t * 8 + j
                keep = lanes < width - d
                shifted = pltpu.roll(jnp.where(keep, main_s[...], spill_s[...]), d, 2)
                volume = jnp.sum(left * shifted, axis=0) * inv
                weighted = (volume - target_ref[g, d].astype(F32)) * inv
                left_grad = left_grad + weighted * shifted
                back = pltpu.roll(weighted * left, lax.rem(width - d, width), 2)
                main_grad = main_grad + jnp.where(keep, back, 0.0)
                spill_grad = spill_grad + jnp.where(keep, 0.0, back)
            return left_grad, main_grad, spill_grad

        zero = jnp.zeros((size, tile_w, width), F32)
        left_grad, main_grad, spill_grad = lax.fori_loop(0, disp // 8, step, (zero, zero, zero))
        left_grad_ref[chans] = left_grad
        own_ref[chans] = main_grad * main_in[0]
        for k in range(1, REACH + 1):
            piece = spill_grad * spill_in[k - 1]
            if k < REACH:
                piece = piece + main_grad * main_in[k]
            out_ref[k - 1, chans] = piece.astype(BF16)
        return carry

    lax.fori_loop(0, groups, one_group, 0)
    fill_views(
        views_ref,
        place,
        lambda n, x: image_ref[n, x].astype(F32),
        lambda side, n: side_ref[side, n].astype(F32),
        lambda j: edges_ref[j].astype(F32),
        images,
        tile_w,
        lane_index((channels, width)),
    )
    for n in range(images):
        for x in range(tile_w):
            view = views_ref[n, x : x + 3].reshape(9 * channels, width)
            total = jnp.dot(w_ref[...], view, preferred_element_type=F32)
            hidden_ref[n, x] = jnp.maximum(total, 0.0).astype(BF16)


def gather_kernel(
    sizes, left_grad_ref, own_ref, out_ref, grad_ref, full_ref, edges_ref, side_ref,
    arrived, rounded, pack, send_sem, recv_sem,
):
    place = Place(sizes)
    local, tile_w, width = own_ref.shape
    images = 2
    chan = place.at["chan"]
    chans = sizes["chan"]
    back = [{"row": -k} for k in range(1, REACH + 1)]
    moves = []
    for dchan in range(1, chans):
        moves.append(("full", None, {"chan": dchan}))
    for dchan in range(chans):
        for side, dc in ((0, 1), (1, -1)):
            moves.append(("side", side, {"col": dc, "chan": dchan}))
    for dchan in range(chans):
        for j, (dr, dc) in enumerate(SIDES):
            moves.append(("edges", j, {"row": -dr, "col": -dc, "chan": dchan}))
    greet(place, back + [move for _, _, move in moves])
    copies = []
    for k in range(REACH):
        copies.append(send(place, back[k], out_ref.at[k], arrived.at[k], send_sem, recv_sem, k))
    left_grad = left_grad_ref[...].astype(BF16)
    grad_ref[0] = left_grad
    rounded[0] = left_grad.astype(F32)
    for x in range(tile_w):
        full_ref[chan, 0, x] = rounded[0, :, x, :].astype(BF16)
    for copy in copies:
        copy.wait()
    right_grad = own_ref[...]
    for k in range(REACH):
        right_grad = right_grad + arrived[k].astype(F32)
    right_grad = right_grad.astype(BF16)
    grad_ref[1] = right_grad
    rounded[1] = right_grad.astype(F32)
    for x in range(tile_w):
        full_ref[chan, 1, x] = rounded[1, :, x, :].astype(BF16)
    copies = []
    packed = False
    for at, (kind, index, move) in enumerate(moves, REACH):
        if kind == "full":
            src, dst = full_ref.at[chan], full_ref.at[chan]
        elif kind == "side":
            x = tile_w - 1 if index == 0 else 0
            src, dst = full_ref.at[chan, :, x], side_ref.at[index, :, chan]
        else:
            if not packed:
                pack[...] = packed_edges(
                    lambda n, x: rounded[n, :, x, :], images, tile_w, lane_index((local, width))
                ).astype(BF16)
                packed = True
            src, dst = pack, edges_ref.at[index, chan]
        copies.append(send(place, move, src, dst, send_sem, recv_sem, at))
    for copy in copies:
        copy.wait()


def weights_kernel(
    sizes, full_ref, edges_ref, side_ref, hidden_ref, input_views, w_ref, out_ref, views_ref
):
    place = Place(sizes)
    chans, images, tile_w, local, width = full_ref.shape
    channels = chans * local

    def joined(parts):
        return jnp.concatenate([p.astype(F32) for p in parts], axis=0)

    fill_views(
        views_ref,
        place,
        lambda n, x: joined([full_ref[c, n, x] for c in range(chans)]),
        lambda side, n: joined([side_ref[side, n, c] for c in range(chans)]),
        lambda j: joined([edges_ref[j, c] for c in range(chans)]),
        images,
        tile_w,
        lane_index((channels, width)),
    )
    contract = (((1,), (1,)), ((), ()))
    first = jnp.zeros((local, 9 * channels), F32)
    second = jnp.zeros((local, 9 * channels), F32)
    for n in range(images):
        for x in range(tile_w):
            view = views_ref[n, x : x + 3].reshape(9 * channels, width)
            hidden = hidden_ref[n, x]
            total = jnp.dot(w_ref[...], view, preferred_element_type=F32)
            hidden_grad = jnp.where(hidden.astype(F32) > 0, total, 0.0).astype(BF16)
            second += lax.dot_general(hidden, view, contract, preferred_element_type=F32)
            image = input_views[n, x : x + 3].reshape(9 * channels, width)
            first += lax.dot_general(hidden_grad, image, contract, preferred_element_type=F32)
    pixels = images * tile_w * sizes["col"] * width * sizes["row"]
    factor = 1.0 / math.sqrt(pixels)
    out_ref[:local] = first * factor
    out_ref[local:] = second * factor


def reduce_kernel(sizes, part_ref, out_ref, arrived, send_sem, recv_sem):
    place = Place(sizes)
    cols = sizes["col"]
    group = sizes["row"] * cols
    rows = part_ref.shape[0] // group
    chan = place.at["chan"]
    me = place.at["row"] * cols + place.at["col"]
    partner = {"chan": lax.rem(chan + 1, sizes["chan"])}

    def peer(by):
        rank = lax.rem(me + by + group, group)
        return rank, {"row": lax.div(rank, cols), "col": lax.rem(rank, cols)}

    def chunk(rank):
        return pl.ds(pl.multiple_of(rank * rows, rows), rows)

    barrier = pltpu.get_barrier_semaphore()
    for by in range(1, group):
        pl.semaphore_signal(barrier, inc=1, device_id=peer(-by)[1], device_id_type=MESH)
    pl.semaphore_signal(barrier, inc=1, device_id=partner, device_id_type=MESH)
    pl.semaphore_wait(barrier, group)

    def start(src, dst, at, device):
        copy = pltpu.make_async_remote_copy(
            src_ref=src, dst_ref=dst, send_sem=send_sem.at[at], recv_sem=recv_sem.at[at],
            device_id=device, device_id_type=MESH,
        )
        copy.start()
        return copy

    scattered = []
    for by in range(1, group):
        rank, device = peer(by)
        scattered.append(start(part_ref.at[chunk(rank)], arrived.at[by - 1], by - 1, device))
    total = part_ref[chunk(me)]
    for by in range(1, group):
        scattered[by - 1].wait()
        total = total + arrived[by - 1]
    out_ref[chan, chunk(me)] = total
    gathered = []
    mine = out_ref.at[chan, chunk(me)]
    for by in range(1, group):
        gathered.append(start(mine, mine, group - 1 + by - 1, peer(by)[1]))
    base = 2 * (group - 1)
    relayed = [start(mine, mine, base, partner)]
    for by in range(1, group):
        gathered[by - 1].wait()
        held = out_ref.at[chan, chunk(peer(-by)[0])]
        relayed.append(start(held, held, base + by, partner))
    for copy in relayed:
        copy.wait()


def body(sizes, layer_input, features, vol_target, offsets, w_first, w_second):
    images, channels, tile_w, width = layer_input.shape
    local = features.shape[1]
    chans = sizes["chan"]
    shape = jax.ShapeDtypeStruct
    dma = pltpu.SemaphoreType.DMA
    first_ch = lax.axis_index("chan") * local
    limit = 48 * 1024 * 1024

    def call(kernel, out_shape, scratch, operands, collective_id=None, specs=None):
        params = {"vmem_limit_bytes": limit}
        if collective_id is not None:
            params.update(collective_id=collective_id, has_side_effects=True)
        return pl.pallas_call(
            functools.partial(kernel, sizes),
            out_shape=out_shape,
            in_specs=specs or [vmem()] * len(operands),
            out_specs=jax.tree.map(lambda _: vmem(), out_shape),
            scratch_shapes=scratch,
            compiler_params=pltpu.CompilerParams(**params),
        )(*operands)

    image = layer_input.transpose(0, 2, 1, 3)
    w1 = lax.dynamic_slice_in_dim(w_first, first_ch, local, 0)
    w1 = w1.transpose(0, 2, 3, 1).reshape(local, 9 * channels)
    w2 = lax.dynamic_slice_in_dim(w_second, first_ch, local, 1)
    w2 = w2[:, :, ::-1, ::-1].transpose(1, 2, 3, 0).reshape(local, 9 * channels)

    count = REACH + 2 + len(SIDES)
    window, edges, side = call(
        fetch_kernel,
        [
            shape((REACH, local, tile_w, width), BF16),
            shape((len(SIDES), channels, width), BF16),
            shape((2, images, channels, width), BF16),
        ],
        [pltpu.VMEM((channels, width), BF16), dma((count,)), dma((count,))],
        (features[1], image),
        0,
    )
    views_shape = (images, tile_w + 2, 3, channels, width)
    size = local // vol_target.shape[0]
    left_grad, own, outgoing, hidden, input_views = call(
        correlate_kernel,
        [
            shape((local, tile_w, width), F32),
            shape((local, tile_w, width), F32),
            shape((REACH, local, tile_w, width), BF16),
            shape((images, tile_w, local, width), BF16),
            shape(views_shape, BF16),
        ],
        [pltpu.VMEM((size, tile_w, width), F32)] * 2,
        (offsets, features[0], features[1], window, vol_target, image, edges, side, w1),
        specs=[pl.BlockSpec(memory_space=pltpu.SMEM)] + [vmem()] * 8,
    )
    count = REACH + (chans - 1) + chans * (2 + len(SIDES))
    grad_features, full, grad_edges, grad_side = call(
        gather_kernel,
        [
            shape((2, local, tile_w, width), BF16),
            shape((chans, 2, tile_w, local, width), BF16),
            shape((len(SIDES), chans, local, width), BF16),
            shape((2, 2, chans, local, width), BF16),
        ],
        [
            pltpu.VMEM((REACH, local, tile_w, width), BF16),
            pltpu.VMEM((2, local, tile_w, width), F32),
            pltpu.VMEM((local, width), BF16),
            dma((count,)),
            dma((count,)),
        ],
        (left_grad, own, outgoing),
        1,
    )
    partial = call(
        weights_kernel,
        shape((2 * local, 9 * channels), F32),
        [pltpu.VMEM(views_shape, BF16)],
        (full, grad_edges, grad_side, hidden, input_views, w2),
    )
    group = sizes["row"] * sizes["col"]
    if chans == 2 and (2 * local) % (8 * group) == 0:
        rows = 2 * local // group
        count = 2 * (group - 1) + group
        summed = call(
            reduce_kernel,
            shape((chans, 2 * local, 9 * channels), F32),
            [pltpu.VMEM((group - 1, rows, 9 * channels), F32), dma((count,)), dma((count,))],
            (partial,),
            2,
        )
    else:
        summed = lax.all_gather(lax.psum(partial, ("row", "col")), "chan")
    first = summed[:, :local].reshape(channels, 3, 3, channels).transpose(0, 3, 1, 2)
    second = summed[:, local:].reshape(channels, 3, 3, channels)[:, ::-1, ::-1]
    return grad_features, first, second.transpose(3, 0, 1, 2)


def solution(mesh):
    return jax.shard_map(
        functools.partial(body, dict(mesh.shape)),
        mesh=mesh,
        in_specs=(
            P(None, None, ("groups", "col"), "row"),
            P(None, "chan", ("groups", "col"), "row"),
            P("chan", None, ("groups", "col"), "row"),
            P("row", ("groups", "col")),
            P(),
            P(),
        ),
        out_specs=(
            P(None, "chan", ("groups", "col"), "row"),
            P("groups", None, None, None),
            P("groups", None, None, None),
        ),
        check_vma=False,
    )
```

time: 375 us -> 60.8 us (0.16)
  local copies, waits for them, and re-layouts: 191 us -> 5.58 us
  waiting for transfers between devices: 117 us -> 0 us
  Pallas kernels: 0 us -> 53.6 us
  starting transfers between devices: 20.8 us -> 0 us
  between operations: 15.2 us -> 1.43 us
  other arithmetic: 12.7 us -> 0 us
  matrix products: 10.3 us -> 0 us
  blocking collectives: 4.97 us -> 0 us
    dynamic_update_slice x42 -> x0, local copies, waits for them, and re-layouts: 189 us -> none  [the longest x40 189 us: one_turn(): lax.dynamic_update_slice_in_dim(window_grad, window_part, first_row, 2)]
    psum x1 -> x0, waiting for transfers between devices: 89.4 us -> none  [body(): lax.psum((first_full, second_full), ('row', 'col', 'chan'))]
    pallas_call x0 -> x5, Pallas kernels: none -> 53.6 us  [call(): pl.pallas_call(functools.partial(kernel, sizes), out_shape=out_shape, in_...]
    ppermute x10 -> x0, waiting for transfers between devices: 27.5 us -> none  [the longest x6 10.7 us: passed_along(): return lax.ppermute(block, axis, route)]
    ppermute x10 -> x0, starting transfers between devices: 20.8 us -> none  [the longest x6 13.4 us: passed_along(): return lax.ppermute(block, axis, route)]
    dot_general x36 -> x0, matrix products: 10.3 us -> none  [the longest x9 3.22 us: recompute_hidden(): jnp.einsum('oi,nixy->noxy', w_first[:, :, a, b], input_halo[:, :, a:a + t...]
    add x46 -> x0, other arithmetic: 5.92 us -> none  [the longest x40 4.36 us: one_turn(): lax.dynamic_slice_in_dim(window_grad, first_row, block_rows, 2)]
    all_gather x1 -> x0, blocking collectives: 4.97 us -> none  [body(): grad_maps = lax.all_gather(grad_features, 'chan', axis=1, tiled=True)]
  transfers between devices with their start and end apart: 11 -> 0, of which waited for: 7 -> 0; matrix products, arithmetic and copies ran while one was open for 1% -> 0% of each run, Pallas kernels for 0% -> 0%
where the time goes in v1:
time: 60.8 us; the launch traced here: 60.6 us
  Pallas kernels  53.6 us (88%)
  local copies, waits for them, and re-layouts  5.58 us (9%)
  between operations  1.43 us (2%)
    pallas_call x5, Pallas kernels, call(): pl.pallas_call(functools.partial(kernel, sizes), out_shape=out_shape, in_...  53.6 us
    unnamed x14, local copies, waits for them, and re-layouts  4.04 us

profile of v1, /device:TPU:1, one launch (start us, length us, event | category | flops | bytes accessed | tf_op | source)
XLA Modules:
  0.0 60.6 jit_solution(15321469744558242017)
XLA Ops:
  0.6 0.0 copy-start
  0.6 0.9 %copy-done = bf16[64,64,3,3]{1,0,3,2:T(8,128)(2,1)S(1)} copy-done((bf16[64,64,3,3]{1,0,3,2:T(8,128)(2,1)S(1)}, bf16[64,64,3,3]{1,0,3,2:T(8,128)(2,1)}, u32[]{:S(2)}) %copy-start) | copy-done | bytes 73752
  1.5 0.0 copy-start.4
  1.6 0.0 copy-start.2
  1.6 0.1 copy.15
  1.6 0.1 reshape.18.w_ref
  1.8 0.7 %copy-done.4 = bf16[2,32,8,128]{3,2,1,0:T(8,128)(2,1)S(1)} copy-done((bf16[2,32,8,128]{3,2,1,0:T(8,128)(2,1)S(1)}, bf16[2,32,8,128]{3,2,1,0:T(8,128)(2,1)}, u32[]{:S(2)}) %copy-start.4) | copy-done | bytes 131096
  2.5 0.1 copy-done.2
  2.6 0.0 copy-start.1
  2.6 12.8 %shard_map.85 = (bf16[3,32,8,128]{3,2,1,0:T(8,128)(2,1)S(1)}, bf16[6,64,128]{2,1,0:T(8,128)(2,1)S(1)}, bf16[2,2,64,128]{3,2,1,0:T(8,128)(2,1)S(1)}) custom-call(bf16[32,8,128]{2,1,0:T(8,128)(2,1)S(1)} %get-tuple-element.32.right_ref, bf16[2,8,64,128]{3,2,1,0:T(8,128)(2,1)S(1)} %bitcast.14), custom_call_target="tpu_custom_call" | custom-call | tf_op jit(solution)/shard_map/pallas_call | solution.py:359
  16.1 0.0 copy-done.1
  16.1 6.4 %shard_map.86 = (f32[32,8,128]{2,1,0:T(8,128)S(1)}, f32[32,8,128]{2,1,0:T(8,128)S(1)}, bf16[3,32,8,128]{3,2,1,0:T(8,128)(2,1)S(1)}, bf16[2,8,32,128]{3,2,1,0:T(8,128)(2,1)S(1)}, bf16[2,10,3,64,128]{4,3,2,1,0:T(8,128)(2,1)S(1)}) custom-call(s32[1,1]{1,0:T(1,128)S(6)} %copy.23.offset_ref, bf16[32,8,128]{2,1,0:T(8,128)(2,1)S(1)} %get-tuple-element.33.left_ref, ...), custom_call_target="tpu_custom_call" | custom-call | tf_op jit(solution)/shard_map/pallas_call | solution.py:359
  22.5 0.0 copy-start.3
  22.5 16.0 %shard_map.87 = (bf16[2,32,8,128]{3,2,1,0:T(8,128)(2,1)S(1)}, bf16[2,2,8,32,128]{4,3,2,1,0:T(8,128)(2,1)S(1)}, bf16[6,2,32,128]{3,2,1,0:T(8,128)(2,1)S(1)}, bf16[2,2,2,32,128]{4,3,2,1,0:T(8,128)(2,1)S(1)}) custom-call(f32[32,8,128]{2,1,0:T(8,128)S(1)} %get-tuple-element.18.left_grad_ref, f32[32,8,128]{2,1,0:T(8,128)S(1)} %get-tuple-element.19.own_ref, ...), custom_call_target="tpu_custom_call" | custom-call | tf_op jit(solution)/shard_map/pallas_call | solution.py:359
  38.5 0.0 copy-done.3
  38.5 0.1 constant_dynamic-slice_fusion
  38.6 0.1 copy.19.w_ref
  38.8 2.9 %shard_map.88.part_ref = f32[64,576]{1,0:T(8,128)S(1)} custom-call(bf16[2,2,8,32,128]{4,3,2,1,0:T(8,128)(2,1)S(1)} %get-tuple-element.22.full_ref, bf16[6,2,32,128]{3,2,1,0:T(8,128)(2,1)S(1)} %get-tuple-element.23.edges_ref, bf16[2,2,2,32,128]{4,3,2,1,0:T(8,128)(2,1)S(1)} %get-tuple-element.24.side_ref, ...), custom_call_target="tpu_custom_call" | custom-call | tf_op jit(solution)/shard_map/pallas_call | solution.py:359
  41.7 15.5 %shard_map.89 = f32[2,64,576]{2,1,0:T(8,128)S(1)} custom-call(f32[64,576]{1,0:T(8,128)S(1)} %shard_map.88.part_ref), custom_call_target="tpu_custom_call" | custom-call | tf_op jit(solution)/shard_map/pallas_call | solution.py:359
  57.2 0.2 reshape.21
  57.4 0.7 %rev.7 = f32[64,3,3,64]{3,2,1,0:T(4,128)S(1)} reverse(f32[64,3,3,64]{3,2,1,0:T(4,128)S(1)} %reshape.21), dimensions={1,2} | reverse | bytes 294912 | tf_op jit(solution)/shard_map/rev | solution.py:440
  58.1 0.9 %copy.18 = f32[64,64,3,3]{1,0,3,2:T(8,128)} copy(f32[64,64,3,3]{0,3,2,1:T(4,128)S(1)} %bitcast.16) | data formatting | bytes 294912
  59.0 0.2 reshape.20
  59.2 0.7 %copy.17 = f32[64,64,3,3]{1,0,3,2:T(8,128)} copy(f32[64,64,3,3]{1,3,2,0:T(4,128)S(1)} %bitcast.17) | data formatting | bytes 294912
  59.9 0.7 %copy.24 = bf16[2,32,8,128]{3,2,1,0:T(8,128)(2,1)} copy(bf16[2,32,8,128]{3,2,1,0:T(8,128)(2,1)S(1)} %get-tuple-element.37) | data formatting | bytes 262144
  (5 shorter events, 0.1 us)
Async XLA Ops:
  0.6 0.9 %copy-start = (bf16[64,64,3,3]{1,0,3,2:T(8,128)(2,1)S(1)}, bf16[64,64,3,3]{1,0,3,2:T(8,128)(2,1)}, u32[]{:S(2)}) copy-start(bf16[64,64,3,3]{1,0,3,2:T(8,128)(2,1)} %param.10) | copy-start | bytes 221188
  1.5 0.9 %copy-start.4 = (bf16[2,32,8,128]{3,2,1,0:T(8,128)(2,1)S(1)}, bf16[2,32,8,128]{3,2,1,0:T(8,128)(2,1)}, u32[]{:S(2)}) copy-start(bf16[2,32,8,128]{3,2,1,0:T(8,128)(2,1)} %param.7) | copy-start | bytes 393220
  1.6 1.0 %copy-start.2 = (bf16[2,64,8,128]{3,2,1,0:T(8,128)(2,1)S(1)}, bf16[2,64,8,128]{3,2,1,0:T(8,128)(2,1)}, u32[]{:S(2)}) copy-start(bf16[2,64,8,128]{3,2,1,0:T(8,128)(2,1)} %param.6) | copy-start | bytes 786436
  2.6 13.5 %copy-start.1 = (bf16[4,40,8,128]{3,2,1,0:T(8,128)(2,1)S(1)}, bf16[4,40,8,128]{3,2,1,0:T(8,128)(2,1)}, u32[]{:S(2)}) copy-start(bf16[4,40,8,128]{3,2,1,0:T(8,128)(2,1)} %target_ref.1) | copy-start | bytes 983044
  22.5 16.0 %copy-start.3 = (bf16[64,64,3,3]{1,0,3,2:T(8,128)(2,1)S(1)}, bf16[64,64,3,3]{1,0,3,2:T(8,128)(2,1)}, u32[]{:S(2)}) copy-start(bf16[64,64,3,3]{1,0,3,2:T(8,128)(2,1)} %param.11) | copy-start | bytes 221188

commit v2 on v0

v2 whole, which is shorter than its diff:
```python
import functools
import math

import jax
import jax.numpy as jnp
from jax import lax
from jax.experimental import pallas as pl
from jax.experimental.pallas import tpu as pltpu
from jax.sharding import PartitionSpec as P

MAXOFF = 2
REACH = MAXOFF + 1
MESH = pl.DeviceIdType.MESH
SIDES = [(dr, dc) for dr in (-1, 1) for dc in (-1, 0, 1)]
F32 = jnp.float32
BF16 = jnp.bfloat16


def vmem():
    return pl.BlockSpec(memory_space=pltpu.VMEM)


def rolled(value, by):
    by = by % value.shape[-1]
    return value if by == 0 else pltpu.roll(value, by, value.ndim - 1)


def lane_index(shape):
    return lax.broadcasted_iota(jnp.int32, shape, len(shape) - 1)


def either(condition, value, lanes):
    start = jnp.where(condition, 0, lanes.shape[-1])
    return jnp.where(lanes >= start, value, 0.0)


class Links:
    def __init__(self, sizes, send_sem, recv_sem):
        self.sizes = sizes
        self.at = {axis: lax.axis_index(axis) for axis in sizes}
        self.send_sem, self.recv_sem = send_sem, recv_sem
        self.used = 0

    def exists(self, move):
        found = None
        for axis, by in move.items():
            if axis == "chan" or by == 0:
                continue
            there = self.at[axis] + by
            here = jnp.logical_and(there >= 0, there < self.sizes[axis])
            found = here if found is None else jnp.logical_and(found, here)
        return found

    def where(self, move):
        return {
            axis: lax.rem(self.at[axis] + (by + self.sizes[axis]), self.sizes[axis])
            for axis, by in move.items()
        }

    def when(self, move, action):
        found = self.exists(move)
        if found is None:
            action()
        else:
            pl.when(found)(action)

    def back(self, move):
        return {axis: -by for axis, by in move.items()}

    def greet(self, moves, group):
        barrier = pltpu.get_barrier_semaphore()
        count = 0
        for move in moves:
            origin = self.back(move)
            self.when(
                origin,
                lambda origin=origin: pl.semaphore_signal(
                    barrier, inc=1, device_id=self.where(origin), device_id_type=MESH
                ),
            )
            found = self.exists(move)
            count = count + (1 if found is None else found.astype(jnp.int32))
        for by in range(1, group):
            device = self.peer(-by, group)[1]
            pl.semaphore_signal(barrier, inc=1, device_id=device, device_id_type=MESH)
            count = count + 1
        pl.semaphore_wait(barrier, count)

    def peer(self, by, group):
        cols = self.sizes["col"]
        me = self.at["row"] * cols + self.at["col"]
        rank = lax.rem(me + by + group, group)
        return rank, {"row": lax.div(rank, cols), "col": lax.rem(rank, cols)}

    def copy(self, src, dst, device):
        at = self.used
        self.used += 1
        return pltpu.make_async_remote_copy(
            src_ref=src,
            dst_ref=dst,
            send_sem=self.send_sem.at[at],
            recv_sem=self.recv_sem.at[at],
            device_id=device,
            device_id_type=MESH,
        )

    def send(self, move, src, dst):
        copy = self.copy(src, dst, self.where(move))
        self.when(move, copy.start)
        return move, copy

    def received(self, sent):
        for move, copy in sent:
            self.when(self.back(move), copy.wait_recv)

    def left(self, sent):
        for move, copy in sent:
            self.when(move, copy.wait_send)


def packed_edges(tiles, lanes):
    packed = jnp.zeros(lanes.shape, F32)
    for k, tile in enumerate(tiles):
        packed = jnp.where(lanes == k, rolled(tile, k + 1), packed)
        packed = jnp.where(lanes == len(tiles) + k, rolled(tile, len(tiles) + k), packed)
    return packed


def fill_views(views, links, n, tile_of, side_of, edges_of, tile_w, lanes):
    width = lanes.shape[1]
    for dc in (-1, 0, 1):
        before = either(
            links.exists({"row": -1, "col": dc}), edges_of(SIDES.index((-1, dc))), lanes
        )
        after = either(links.exists({"row": 1, "col": dc}), edges_of(SIDES.index((1, dc))), lanes)
        for xx in {-1: [0], 0: range(1, tile_w + 1), 1: [tile_w + 1]}[dc]:
            if dc == 0:
                tile, k = tile_of(xx - 1), xx - 1
            else:
                tile = either(links.exists({"col": dc}), side_of(0 if dc < 0 else 1), lanes)
                k = tile_w - 1 if dc < 0 else 0
            left = jnp.where(lanes == 0, rolled(before, -k), rolled(tile, 1))
            right = jnp.where(
                lanes == width - 1, rolled(after, width - 1 - tile_w - k), rolled(tile, -1)
            )
            views[n, xx, 0] = left.astype(BF16)
            views[n, xx, 1] = tile.astype(BF16)
            views[n, xx, 2] = right.astype(BF16)


EDGE_MOVES = [{"row": -dr, "col": -dc} for dr, dc in SIDES]
SIDE_MOVES = [{"col": 1}, {"col": -1}]


def whole_kernel(
    sizes, group, offset_ref, features_ref, target_ref, image_ref, w1_ref, w2_ref,
    grad_ref, sum_ref,
    image, image_pack, image_edges, image_side, image_views, hidden_s, w1, w2, turned, turned_w,
    window, main_s, spill_s, outgoing, arrived, own, rounded, full, grad_pack, grad_edges,
    grad_side, grad_views, part, parts, send_sem, recv_sem,
):
    links = Links(sizes, send_sem, recv_sem)
    images, channels, tile_w, width = image_ref.shape
    local = features_ref.shape[1]
    groups, disp = target_ref.shape[:2]
    size = local // groups
    inv = 1.0 / size
    chans = sizes["chan"]
    chan = links.at["chan"]
    row = links.at["row"]
    direct = group > 0
    forward = [{"row": k} for k in range(1, REACH + 1)]
    backward = [{"row": -k} for k in range(1, REACH + 1)]
    with_chan = [{**move, "chan": c} for move in EDGE_MOVES + SIDE_MOVES for c in range(chans)]
    partners = [{"chan": c} for c in range(1, chans)]
    links.greet(forward + backward + with_chan + partners, group)
    pending = []

    def parts_of(g):
        return pl.ds(g * size, size)

    fetched = []
    for g in range(groups):
        fetched.append([
            links.send(
                forward[k], features_ref.at[1, parts_of(g)], window.at[k, parts_of(g)]
            )
            for k in range(REACH)
        ])
        pending += fetched[-1]

    lanes = lane_index((channels, width))
    for n in range(images):
        turned[...] = image_ref[n].astype(F32)
        for x in range(tile_w):
            image[n, x] = turned[:, x, :].astype(BF16)
    border = [
        links.send(move, image.at[:, x], image_side.at[side])
        for side, (x, move) in enumerate(zip((tile_w - 1, 0), SIDE_MOVES))
    ]
    for n in range(images):
        image_pack[n] = packed_edges(
            [image[n, x].astype(F32) for x in range(tile_w)], lanes
        ).astype(BF16)
    border += [
        links.send(move, image_pack, image_edges.at[j]) for j, move in enumerate(EDGE_MOVES)
    ]
    pending += border

    first_ch = pl.multiple_of(chan * local, local)
    mine = pl.ds(first_ch, local)
    taps = [(a, b) for a in range(3) for b in range(3)]
    w1[...] = jnp.concatenate([w1_ref[a, b, mine].astype(F32) for a, b in taps], axis=1).astype(BF16)
    flipped = jnp.concatenate([w2_ref[2 - a, 2 - b].astype(F32) for a, b in taps], axis=0)
    turned_w[...] = flipped.T
    w2[...] = turned_w[mine].astype(BF16)

    links.received(border)
    for n in range(images):
        fill_views(
            image_views, links, n,
            lambda x, n=n: image[n, x].astype(F32),
            lambda side, n=n: image_side[side, n].astype(F32),
            lambda j, n=n: image_edges[j, n].astype(F32),
            tile_w, lanes,
        )
    for n in range(images):
        for x in range(tile_w):
            view = image_views[n, x : x + 3].reshape(9 * channels, width)
            total = jnp.dot(w1[...], view, preferred_element_type=F32)
            hidden_s[n, x] = jnp.maximum(total, 0.0).astype(BF16)

    small = lane_index((tile_w, width))
    offset = jnp.broadcast_to(offset_ref[...], (tile_w, width))
    inside = small * 0 + row
    main_in = [offset == k for k in range(REACH)]
    spill_in = [
        jnp.logical_and(offset + 1 == k, inside >= k) for k in range(1, REACH + 1)
    ]
    returned = []
    for g in range(groups):
        links.received(fetched[g])
        chosen = parts_of(g)
        main = jnp.where(main_in[0], features_ref[1, chosen].astype(F32), 0.0)
        spill = jnp.zeros_like(main)
        for k in range(REACH):
            got = window[k, chosen].astype(F32)
            spill = jnp.where(spill_in[k], got, spill)
            if k + 1 < REACH:
                main = jnp.where(main_in[k + 1], got, main)
        main_s[...] = main
        spill_s[...] = spill

        def step(t, state, g=g, chosen=chosen):
            left_grad, main_grad, spill_grad = state
            left = features_ref[0, chosen].astype(F32)
            for j in range(8):
                d = t * 8 + j
                keep = small < width - d
                shifted = pltpu.roll(jnp.where(keep, main_s[...], spill_s[...]), d, 2)
                volume = jnp.sum(left * shifted, axis=0) * inv
                weighted = (volume - target_ref[g, d].astype(F32)) * inv
                left_grad = left_grad + weighted * shifted
                back = pltpu.roll(weighted * left, lax.rem(width - d, width), 2)
                main_grad = main_grad + jnp.where(keep, back, 0.0)
                spill_grad = spill_grad + jnp.where(keep, 0.0, back)
            return left_grad, main_grad, spill_grad

        zero = jnp.zeros((size, tile_w, width), F32)
        left_grad, main_grad, spill_grad = lax.fori_loop(0, disp // 8, step, (zero, zero, zero))
        for k in range(1, REACH + 1):
            piece = jnp.where(spill_in[k - 1], spill_grad, 0.0)
            if k < REACH:
                piece = jnp.where(main_in[k], main_grad, piece)
            outgoing[k - 1, chosen] = piece.astype(BF16)
        returned.append([
            links.send(backward[k], outgoing.at[k, chosen], arrived.at[k, chosen])
            for k in range(REACH)
        ])
        pending += returned[-1]
        own[chosen] = jnp.where(main_in[0], main_grad, 0.0)
        left_grad = left_grad.astype(BF16)
        grad_ref[0, chosen] = left_grad
        rounded[0, chosen] = left_grad.astype(F32)

    slim = lane_index((local, width))

    def share(n):
        for x in range(tile_w):
            full[n, chan, x] = rounded[n, :, x, :].astype(BF16)
        sent = [links.send(move, full.at[n, chan], full.at[n, chan]) for move in partners]
        for c in range(chans):
            for side, (x, move) in enumerate(zip((tile_w - 1, 0), SIDE_MOVES)):
                sent.append(links.send(
                    {**move, "chan": c}, full.at[n, chan, x], grad_side.at[n, side, chan]
                ))
        grad_pack[n] = packed_edges(
            [rounded[n, :, x, :] for x in range(tile_w)], slim
        ).astype(BF16)
        for c in range(chans):
            for j, move in enumerate(EDGE_MOVES):
                sent.append(links.send(
                    {**move, "chan": c}, grad_pack.at[n], grad_edges.at[n, j, chan]
                ))
        return sent

    def joined(pieces):
        return jnp.concatenate([p.astype(F32) for p in pieces], axis=0)

    contract = (((1,), (1,)), ((), ()))

    def gradients(n, first, second):
        fill_views(
            grad_views, links, n,
            lambda x: joined([full[n, c, x] for c in range(chans)]),
            lambda side: joined([grad_side[n, side, c] for c in range(chans)]),
            lambda j: joined([grad_edges[n, j, c] for c in range(chans)]),
            tile_w, lanes,
        )
        for x in range(tile_w):
            view = grad_views[n, x : x + 3].reshape(9 * channels, width)
            hidden = hidden_s[n, x]
            total = jnp.dot(w2[...], view, preferred_element_type=F32)
            hidden_grad = jnp.where(hidden.astype(F32) > 0, total, 0.0).astype(BF16)
            second += lax.dot_general(hidden, view, contract, preferred_element_type=F32)
            seen = image_views[n, x : x + 3].reshape(9 * channels, width)
            first += lax.dot_general(hidden_grad, seen, contract, preferred_element_type=F32)
        return first, second

    left_sent = share(0)
    for g in range(groups):
        links.received(returned[g])
        chosen = parts_of(g)
        right_grad = own[chosen]
        for k in range(REACH):
            there = inside + (k + 1) < sizes["row"]
            right_grad = right_grad + jnp.where(there, arrived[k, chosen].astype(F32), 0.0)
        right_grad = right_grad.astype(BF16)
        grad_ref[1, chosen] = right_grad
        rounded[1, chosen] = right_grad.astype(F32)
    right_sent = share(1)
    pending += left_sent + right_sent
    empty = jnp.zeros((local, 9 * channels), F32)
    links.received(left_sent)
    first, second = gradients(0, empty, empty)
    links.received(right_sent)
    first, second = gradients(1, first, second)
    pixels = images * tile_w * sizes["col"] * width * sizes["row"]
    factor = 1.0 / math.sqrt(pixels)
    first, second = first * factor, second * factor

    if direct:
        rows = 2 * local // group
        half = group // 2
        for j in range(half):
            part[j] = first[j * rows : (j + 1) * rows].astype(BF16)
            part[half + j] = second[j * rows : (j + 1) * rows].astype(BF16)
        scattered, gathered, relayed = [], [], []
        for by in range(1, group):
            rank, device = links.peer(by, group)
            scattered.append(links.copy(part.at[rank], parts.at[by - 1], device))
            scattered[-1].start()
        me = links.peer(0, group)[0]
        total = part[me].astype(F32)
        for by in range(1, group):
            scattered[by - 1].wait_recv()
            total = total + parts[by - 1].astype(F32)
        sum_ref[chan, me] = total.astype(BF16)
        partner = links.where(partners[0])
        held = sum_ref.at[chan, me]
        for by in range(1, group):
            gathered.append(links.copy(held, held, links.peer(by, group)[1]))
            gathered[-1].start()
        relayed.append(links.copy(held, held, partner))
        relayed[-1].start()
        for by in range(1, group):
            gathered[by - 1].wait_recv()
            held = sum_ref.at[chan, links.peer(-by, group)[0]]
            relayed.append(links.copy(held, held, partner))
            relayed[-1].start()
        for copy in relayed:
            copy.wait_recv()
        for copy in scattered + gathered + relayed:
            copy.wait_send()
    else:
        sum_ref[:local] = first
        sum_ref[local:] = second
    links.left(pending)


def write_kernel(sum_ref, first_ref, second_ref):
    chans, pieces = sum_ref.shape[:2]
    channels = first_ref.shape[1]
    half = pieces // 2

    def rows(pick):
        return jnp.concatenate(
            [sum_ref[c, j].astype(F32) for c in range(chans) for j in pick], axis=0
        )

    first = rows(range(half))
    second = rows(range(half, pieces)).T
    for t in range(9):
        chosen = slice(t * channels, (t + 1) * channels)
        first_ref[t] = first[:, chosen]
        second_ref[8 - t] = second[chosen]


def body(sizes, layer_input, features, vol_target, offsets, w_first, w_second):
    images, channels, tile_w, width = layer_input.shape
    local = features.shape[1]
    chans = sizes["chan"]
    shape = jax.ShapeDtypeStruct
    dma = pltpu.SemaphoreType.DMA
    scratch = pltpu.VMEM
    size = local // vol_target.shape[0]
    group = sizes["row"] * sizes["col"]
    if chans != 2 or group % 2 or (2 * local) % (8 * group):
        group = 0
    rows = 2 * local // max(group, 2)
    views = (images, tile_w + 2, 3, channels, width)
    tile = (local, tile_w, width)
    edge = (len(SIDES), images, channels, width)
    count = 2 * REACH * vol_target.shape[0] + 2 + len(SIDES)
    count += images * ((chans - 1) + chans * (2 + len(SIDES))) + 3 * group
    if group:
        summed_shape = shape((chans, group, rows, 9 * channels), BF16)
    else:
        summed_shape = shape((2 * local, 9 * channels), F32)
    grad_features, summed = pl.pallas_call(
        functools.partial(whole_kernel, sizes, group),
        out_shape=[shape((2,) + tile, BF16), summed_shape],
        in_specs=[vmem()] * 6,
        out_specs=[vmem()] * 2,
        scratch_shapes=[
            scratch((images, tile_w, channels, width), BF16),
            scratch((images, channels, width), BF16),
            scratch(edge, BF16),
            scratch((2, images, channels, width), BF16),
            scratch(views, BF16),
            scratch((images, tile_w, local, width), BF16),
            scratch((local, 9 * channels), BF16),
            scratch((local, 9 * channels), BF16),
            scratch((channels, tile_w, width), F32),
            scratch((channels, 9 * channels), F32),
            scratch((REACH,) + tile, BF16),
            scratch((size, tile_w, width), F32),
            scratch((size, tile_w, width), F32),
            scratch((REACH,) + tile, BF16),
            scratch((REACH,) + tile, BF16),
            scratch(tile, F32),
            scratch((2,) + tile, F32),
            scratch((2, chans, tile_w, local, width), BF16),
            scratch((2, local, width), BF16),
            scratch((2, len(SIDES), chans, local, width), BF16),
            scratch((2, 2, chans, local, width), BF16),
            scratch(views, BF16),
            scratch((max(group, 2), rows, 9 * channels), BF16),
            scratch((max(group, 2), rows, 9 * channels), BF16),
            dma((count,)),
            dma((count,)),
        ],
        compiler_params=pltpu.CompilerParams(
            collective_id=0, has_side_effects=True, vmem_limit_bytes=48 * 1024 * 1024
        ),
    )(
        offsets,
        features,
        vol_target,
        layer_input,
        w_first.transpose(2, 3, 0, 1),
        w_second.transpose(2, 3, 0, 1),
    )
    if not group:
        summed = lax.all_gather(lax.psum(summed, ("row", "col")), "chan")
        summed = summed.reshape(chans, 2, local, 9 * channels)
    first, second = pl.pallas_call(
        write_kernel,
        out_shape=[shape((9, channels, channels), F32)] * 2,
        in_specs=[vmem()],
        out_specs=[vmem()] * 2,
        compiler_params=pltpu.CompilerParams(vmem_limit_bytes=16 * 1024 * 1024),
    )(summed)
    first = first.reshape(3, 3, channels, channels).transpose(2, 3, 0, 1)
    second = second.reshape(3, 3, channels, channels).transpose(2, 3, 0, 1)
    return grad_features, first, second


def solution(mesh):
    return jax.shard_map(
        functools.partial(body, dict(mesh.shape)),
        mesh=mesh,
        in_specs=(
            P(None, None, ("groups", "col"), "row"),
            P(None, "chan", ("groups", "col"), "row"),
            P("chan", None, ("groups", "col"), "row"),
            P("row", ("groups", "col")),
            P(),
            P(),
        ),
        out_specs=(
            P(None, "chan", ("groups", "col"), "row"),
            P("groups", None, None, None),
            P("groups", None, None, None),
        ),
        check_vma=False,
    )
```

time: 375 us -> 48 us (0.13)
  local copies, waits for them, and re-layouts: 191 us -> 5.29 us
  waiting for transfers between devices: 117 us -> 0 us
  Pallas kernels: 0 us -> 41.1 us
  starting transfers between devices: 20.8 us -> 0 us
  between operations: 15.2 us -> 1.3 us
  other arithmetic: 12.7 us -> 0 us
  matrix products: 10.3 us -> 0 us
  blocking collectives: 4.97 us -> 0 us
    dynamic_update_slice x42 -> x0, local copies, waits for them, and re-layouts: 189 us -> none  [the longest x40 189 us: one_turn(): lax.dynamic_update_slice_in_dim(window_grad, window_part, first_row, 2)]
    psum x1 -> x0, waiting for transfers between devices: 89.4 us -> none  [body(): lax.psum((first_full, second_full), ('row', 'col', 'chan'))]
    pallas_call x0 -> x2, Pallas kernels: none -> 41.1 us  [the longest x1 40.1 us: body(): pl.pallas_call(functools.partial(whole_kernel, sizes, group), out_shape=[...]
    ppermute x10 -> x0, waiting for transfers between devices: 27.5 us -> none  [the longest x6 10.7 us: passed_along(): return lax.ppermute(block, axis, route)]
    ppermute x10 -> x0, starting transfers between devices: 20.8 us -> none  [the longest x6 13.4 us: passed_along(): return lax.ppermute(block, axis, route)]
    dot_general x36 -> x0, matrix products: 10.3 us -> none  [the longest x9 3.22 us: recompute_hidden(): jnp.einsum('oi,nixy->noxy', w_first[:, :, a, b], input_halo[:, :, a:a + t...]
    add x46 -> x0, other arithmetic: 5.92 us -> none  [the longest x40 4.36 us: one_turn(): lax.dynamic_slice_in_dim(window_grad, first_row, block_rows, 2)]
    all_gather x1 -> x0, blocking collectives: 4.97 us -> none  [body(): grad_maps = lax.all_gather(grad_features, 'chan', axis=1, tiled=True)]
  transfers between devices with their start and end apart: 11 -> 0, of which waited for: 7 -> 0; matrix products, arithmetic and copies ran while one was open for 1% -> 0% of each run, Pallas kernels for 0% -> 0%
where the time goes in v2:
time: 48 us; the launch traced here: 47.7 us
  Pallas kernels  41.1 us (86%)
  local copies, waits for them, and re-layouts  5.29 us (11%)
  between operations  1.3 us (3%)
    pallas_call x1, Pallas kernels, body(): pl.pallas_call(functools.partial(whole_kernel, sizes, group), out_shape=[...  40.1 us
    unnamed x11, local copies, waits for them, and re-layouts  5.29 us

profile of v2, /device:TPU:1, one launch (start us, length us, event | category | flops | bytes accessed | tf_op | source)
XLA Modules:
  0.0 47.7 jit_solution(3620785044310538452)
XLA Ops:
  1.3 0.0 copy-start
  1.3 1.0 %copy-done = bf16[4,40,8,128]{3,2,1,0:T(8,128)(2,1)S(1)} copy-done((bf16[4,40,8,128]{3,2,1,0:T(8,128)(2,1)S(1)}, bf16[4,40,8,128]{3,2,1,0:T(8,128)(2,1)}, u32[]{:S(2)}) %copy-start) | copy-done | bytes 327704
  2.3 0.0 copy-start.1
  2.3 0.9 %copy-done.1 = bf16[2,64,8,128]{3,2,1,0:T(8,128)(2,1)S(1)} copy-done((bf16[2,64,8,128]{3,2,1,0:T(8,128)(2,1)S(1)}, bf16[2,64,8,128]{3,2,1,0:T(8,128)(2,1)}, u32[]{:S(2)}) %copy-start.1) | copy-done | bytes 262168
  3.2 0.0 copy-start.2
  3.2 0.9 %copy-done.2 = bf16[64,64,3,3]{1,0,3,2:T(8,128)(2,1)S(1)} copy-done((bf16[64,64,3,3]{1,0,3,2:T(8,128)(2,1)S(1)}, bf16[64,64,3,3]{1,0,3,2:T(8,128)(2,1)}, u32[]{:S(2)}) %copy-start.2) | copy-done | bytes 73752
  4.1 0.0 copy-start.3
  4.1 0.9 %copy-done.3 = bf16[64,64,3,3]{1,0,3,2:T(8,128)(2,1)S(1)} copy-done((bf16[64,64,3,3]{1,0,3,2:T(8,128)(2,1)S(1)}, bf16[64,64,3,3]{1,0,3,2:T(8,128)(2,1)}, u32[]{:S(2)}) %copy-start.3) | copy-done | bytes 73752
  5.0 0.0 copy-start.4
  5.0 0.9 %copy-done.4 = bf16[2,32,8,128]{3,2,1,0:T(8,128)(2,1)S(1)} copy-done((bf16[2,32,8,128]{3,2,1,0:T(8,128)(2,1)S(1)}, bf16[2,32,8,128]{3,2,1,0:T(8,128)(2,1)}, u32[]{:S(2)}) %copy-start.4) | copy-done | bytes 131096
  5.9 40.1 %shard_map.85 = (bf16[2,32,8,128]{3,2,1,0:T(8,128)(2,1)S(1)}, bf16[2,8,8,576]{3,2,1,0:T(8,128)(2,1)S(1)}) custom-call(s32[1,1]{1,0:T(1,128)S(6)} %copy.10.offset_ref, bf16[2,32,8,128]{3,2,1,0:T(8,128)(2,1)S(1)} %copy-done.4, bf16[4,40,8,128]{3,2,1,0:T(8,128)(2,1)S(1)} %copy-done, bf16[2,64,8,128]{3,2,1,0:T(8,128)(2,1)S(1)} %copy-done.1, ...), custom_call_target="tpu_custom_call" | custom-call | tf_op jit(solution)/shard_map/pallas_call | solution.py:430
  46.1 0.9 %shard_map.86 = (f32[9,64,64]{2,1,0:T(8,128)}, f32[9,64,64]{2,1,0:T(8,128)}) custom-call(bf16[2,8,8,576]{3,2,1,0:T(8,128)(2,1)S(1)} %get-tuple-element.8.sum_ref), custom_call_target="tpu_custom_call" | custom-call | tf_op jit(solution)/shard_map/pallas_call | solution.py:477
  47.0 0.7 %copy.11 = bf16[2,32,8,128]{3,2,1,0:T(8,128)(2,1)} copy(bf16[2,32,8,128]{3,2,1,0:T(8,128)(2,1)S(1)} %get-tuple-element.14) | data formatting | bytes 262144
Async XLA Ops:
  1.3 1.0 %copy-start = (bf16[4,40,8,128]{3,2,1,0:T(8,128)(2,1)S(1)}, bf16[4,40,8,128]{3,2,1,0:T(8,128)(2,1)}, u32[]{:S(2)}) copy-start(bf16[4,40,8,128]{3,2,1,0:T(8,128)(2,1)} %target_ref.1) | copy-start | bytes 983044
  2.3 0.9 %copy-start.1 = (bf16[2,64,8,128]{3,2,1,0:T(8,128)(2,1)S(1)}, bf16[2,64,8,128]{3,2,1,0:T(8,128)(2,1)}, u32[]{:S(2)}) copy-start(bf16[2,64,8,128]{3,2,1,0:T(8,128)(2,1)} %image_ref.1) | copy-start | bytes 786436
  3.2 0.9 %copy-start.2 = (bf16[64,64,3,3]{1,0,3,2:T(8,128)(2,1)S(1)}, bf16[64,64,3,3]{1,0,3,2:T(8,128)(2,1)}, u32[]{:S(2)}) copy-start(bf16[64,64,3,3]{1,0,3,2:T(8,128)(2,1)} %param.10) | copy-start | bytes 221188
  4.1 0.9 %copy-start.3 = (bf16[64,64,3,3]{1,0,3,2:T(8,128)(2,1)S(1)}, bf16[64,64,3,3]{1,0,3,2:T(8,128)(2,1)}, u32[]{:S(2)}) copy-start(bf16[64,64,3,3]{1,0,3,2:T(8,128)(2,1)} %param.11) | copy-start | bytes 221188
  5.0 0.9 %copy-start.4 = (bf16[2,32,8,128]{3,2,1,0:T(8,128)(2,1)S(1)}, bf16[2,32,8,128]{3,2,1,0:T(8,128)(2,1)}, u32[]{:S(2)}) copy-start(bf16[2,32,8,128]{3,2,1,0:T(8,128)(2,1)} %features_ref.1) | copy-start | bytes 393220

commit v3 on v2

--- a/solution.py
+++ b/solution.py
@@ -118,30 +118,47 @@
             self.when(move, copy.wait_send)
 
 
-def packed_edges(tiles, lanes):
+def packed_edges(tiles, per):
+    count = len(tiles)
+    rows = tiles[0].shape[0] // per
+    lanes = lane_index((rows, tiles[0].shape[1]))
     packed = jnp.zeros(lanes.shape, F32)
-    for k, tile in enumerate(tiles):
-        packed = jnp.where(lanes == k, rolled(tile, k + 1), packed)
-        packed = jnp.where(lanes == len(tiles) + k, rolled(tile, len(tiles) + k), packed)
+    for q in range(per):
+        first = q * 2 * count
+        for k, tile in enumerate(tiles):
+            piece = tile[q * rows : (q + 1) * rows]
+            packed = jnp.where(lanes == first + k, rolled(piece, first + k + 1), packed)
+            packed = jnp.where(
+                lanes == first + count + k, rolled(piece, first + count + k), packed
+            )
     return packed
 
 
-def fill_views(views, links, n, tile_of, side_of, edges_of, tile_w, lanes):
+def spread(blocks, by, per, count):
+    return jnp.concatenate(
+        [rolled(block, by - q * 2 * count) for block in blocks for q in range(per)], axis=0
+    )
+
+
+def fill_views(views, links, n, tile_of, side_of, edges_of, tile_w, lanes, per, count, first):
     width = lanes.shape[1]
     for dc in (-1, 0, 1):
-        before = either(
-            links.exists({"row": -1, "col": dc}), edges_of(SIDES.index((-1, dc))), lanes
-        )
-        after = either(links.exists({"row": 1, "col": dc}), edges_of(SIDES.index((1, dc))), lanes)
+        before = edges_of(SIDES.index((-1, dc)))
+        after = edges_of(SIDES.index((1, dc)))
+        slim = lane_index(before[0].shape)
+        before = [either(links.exists({"row": -1, "col": dc}), b, slim) for b in before]
+        after = [either(links.exists({"row": 1, "col": dc}), b, slim) for b in after]
         for xx in {-1: [0], 0: range(1, tile_w + 1), 1: [tile_w + 1]}[dc]:
             if dc == 0:
-                tile, k = tile_of(xx - 1), xx - 1
+                tile, k = tile_of(xx - 1), first + xx - 1
             else:
                 tile = either(links.exists({"col": dc}), side_of(0 if dc < 0 else 1), lanes)
-                k = tile_w - 1 if dc < 0 else 0
-            left = jnp.where(lanes == 0, rolled(before, -k), rolled(tile, 1))
+                k = first + (tile_w - 1 if dc < 0 else 0)
+            left = jnp.where(lanes == 0, spread(before, -k, per, count), rolled(tile, 1))
             right = jnp.where(
-                lanes == width - 1, rolled(after, width - 1 - tile_w - k), rolled(tile, -1)
+                lanes == width - 1,
+                spread(after, width - 1 - count - k, per, count),
+                rolled(tile, -1),
             )
             views[n, xx, 0] = left.astype(BF16)
             views[n, xx, 1] = tile.astype(BF16)
@@ -153,11 +170,12 @@
 
 
 def whole_kernel(
-    sizes, group, offset_ref, features_ref, target_ref, image_ref, w1_ref, w2_ref,
-    grad_ref, sum_ref,
+    sizes, group, offset_ref, features_hbm, target_hbm, image_hbm, w1_hbm, w2_hbm,
+    grad_out, sum_out,
+    grad_ref, sum_ref, features_ref, target_ref, image_ref, w1_ref, w2_ref, far_out, far_in, far_back, far_home,
     image, image_pack, image_edges, image_side, image_views, hidden_s, w1, w2, turned, turned_w,
     window, main_s, spill_s, outgoing, arrived, own, rounded, full, grad_pack, grad_edges,
-    grad_side, grad_views, part, parts, send_sem, recv_sem,
+    grad_side, grad_views, part, parts, send_sem, recv_sem, load_sem,
 ):
     links = Links(sizes, send_sem, recv_sem)
     images, channels, tile_w, width = image_ref.shape
@@ -173,8 +191,49 @@
     backward = [{"row": -k} for k in range(1, REACH + 1)]
     with_chan = [{**move, "chan": c} for move in EDGE_MOVES + SIDE_MOVES for c in range(chans)]
     partners = [{"chan": c} for c in range(1, chans)]
+    loads = [
+        pltpu.make_async_copy(src, dst, load_sem.at[i])
+        for i, (src, dst) in enumerate([
+            (features_hbm.at[1], features_ref.at[1]),
+            (image_hbm, image_ref),
+            (w1_hbm, w1_ref),
+            (w2_hbm, w2_ref),
+            (features_hbm.at[0], features_ref.at[0]),
+            (target_hbm, target_ref),
+        ])
+    ]
+    for load in loads:
+        load.start()
+    pending = []
+    lanes = lane_index((channels, width))
+    small = lane_index((tile_w, width))
+    abreast = width // disp
+
+    def packed_far(values, dst, first):
+        for i in range(first, first + -(-size // abreast)):
+            packed = None
+            for r in range(abreast):
+                c = (i - first) * abreast + r
+                if c < size:
+                    value = rolled(values[c], disp + r * disp)
+                    packed = value if r == 0 else jnp.where(small >= r * disp, value, packed)
+            dst[i] = packed.astype(BF16)
+
+    def unpacked_far(src, first):
+        return jnp.stack([
+            rolled(src[first + c // abreast].astype(F32), width - disp - (c % abreast) * disp)
+            for c in range(size)
+        ])
+
+    far = -(-size // abreast)
+
+    def far_of(g):
+        return pl.ds(g * far, far)
+
+    loads[0].wait()
+    for g in range(groups):
+        packed_far(features_ref[1, g * size : (g + 1) * size].astype(F32), far_out, g * far)
     links.greet(forward + backward + with_chan + partners, group)
-    pending = []
 
     def parts_of(g):
         return pl.ds(g * size, size)
@@ -185,11 +244,14 @@
             links.send(
                 forward[k], features_ref.at[1, parts_of(g)], window.at[k, parts_of(g)]
             )
-            for k in range(REACH)
+            for k in range(MAXOFF)
         ])
+        fetched[-1].append(
+            links.send(forward[MAXOFF], far_out.at[far_of(g)], far_in.at[far_of(g)])
+        )
         pending += fetched[-1]
 
-    lanes = lane_index((channels, width))
+    loads[1].wait()
     for n in range(images):
         turned[...] = image_ref[n].astype(F32)
         for x in range(tile_w):
@@ -198,15 +260,18 @@
         links.send(move, image.at[:, x], image_side.at[side])
         for side, (x, move) in enumerate(zip((tile_w - 1, 0), SIDE_MOVES))
     ]
-    for n in range(images):
-        image_pack[n] = packed_edges(
-            [image[n, x].astype(F32) for x in range(tile_w)], lanes
-        ).astype(BF16)
+    count = images * tile_w
+    image_per = channels // image_pack.shape[0]
+    image_pack[...] = packed_edges(
+        [image[n, x].astype(F32) for n in range(images) for x in range(tile_w)], image_per
+    ).astype(BF16)
     border += [
         links.send(move, image_pack, image_edges.at[j]) for j, move in enumerate(EDGE_MOVES)
     ]
     pending += border
 
+    loads[2].wait()
+    loads[3].wait()
     first_ch = pl.multiple_of(chan * local, local)
     mine = pl.ds(first_ch, local)
     taps = [(a, b) for a in range(3) for b in range(3)]
@@ -221,8 +286,8 @@
             image_views, links, n,
             lambda x, n=n: image[n, x].astype(F32),
             lambda side, n=n: image_side[side, n].astype(F32),
-            lambda j, n=n: image_edges[j, n].astype(F32),
-            tile_w, lanes,
+            lambda j: [image_edges[j].astype(F32)],
+            tile_w, lanes, image_per, count, n * tile_w,
         )
     for n in range(images):
         for x in range(tile_w):
@@ -230,7 +295,8 @@
             total = jnp.dot(w1[...], view, preferred_element_type=F32)
             hidden_s[n, x] = jnp.maximum(total, 0.0).astype(BF16)
 
-    small = lane_index((tile_w, width))
+    loads[4].wait()
+    loads[5].wait()
     offset = jnp.broadcast_to(offset_ref[...], (tile_w, width))
     inside = small * 0 + row
     main_in = [offset == k for k in range(REACH)]
@@ -244,7 +310,7 @@
         main = jnp.where(main_in[0], features_ref[1, chosen].astype(F32), 0.0)
         spill = jnp.zeros_like(main)
         for k in range(REACH):
-            got = window[k, chosen].astype(F32)
+            got = window[k, chosen].astype(F32) if k < MAXOFF else unpacked_far(far_in, g * far)
             spill = jnp.where(spill_in[k], got, spill)
             if k + 1 < REACH:
                 main = jnp.where(main_in[k + 1], got, main)
@@ -272,18 +338,23 @@
             piece = jnp.where(spill_in[k - 1], spill_grad, 0.0)
             if k < REACH:
                 piece = jnp.where(main_in[k], main_grad, piece)
-            outgoing[k - 1, chosen] = piece.astype(BF16)
+                outgoing[k - 1, chosen] = piece.astype(BF16)
+            else:
+                packed_far(piece, far_back, g * far)
         returned.append([
             links.send(backward[k], outgoing.at[k, chosen], arrived.at[k, chosen])
-            for k in range(REACH)
+            for k in range(MAXOFF)
         ])
+        returned[-1].append(
+            links.send(backward[MAXOFF], far_back.at[far_of(g)], far_home.at[far_of(g)])
+        )
         pending += returned[-1]
         own[chosen] = jnp.where(main_in[0], main_grad, 0.0)
         left_grad = left_grad.astype(BF16)
         grad_ref[0, chosen] = left_grad
         rounded[0, chosen] = left_grad.astype(F32)
 
-    slim = lane_index((local, width))
+    grad_per = local // grad_pack.shape[1]
 
     def share(n):
         for x in range(tile_w):
@@ -295,7 +366,7 @@
                     {**move, "chan": c}, full.at[n, chan, x], grad_side.at[n, side, chan]
                 ))
         grad_pack[n] = packed_edges(
-            [rounded[n, :, x, :] for x in range(tile_w)], slim
+            [rounded[n, :, x, :] for x in range(tile_w)], grad_per
         ).astype(BF16)
         for c in range(chans):
             for j, move in enumerate(EDGE_MOVES):
@@ -314,8 +385,8 @@
             grad_views, links, n,
             lambda x: joined([full[n, c, x] for c in range(chans)]),
             lambda side: joined([grad_side[n, side, c] for c in range(chans)]),
-            lambda j: joined([grad_edges[n, j, c] for c in range(chans)]),
-            tile_w, lanes,
+            lambda j: [grad_edges[n, j, c].astype(F32) for c in range(chans)],
+            tile_w, lanes, grad_per, tile_w, 0,
         )
         for x in range(tile_w):
             view = grad_views[n, x : x + 3].reshape(9 * channels, width)
@@ -327,6 +398,12 @@
             first += lax.dot_general(hidden_grad, seen, contract, preferred_element_type=F32)
         return first, second
 
+    def save(src, dst, at):
+        copy = pltpu.make_async_copy(src, dst, load_sem.at[at])
+        copy.start()
+        return copy
+
+    saves = [save(grad_ref.at[0], grad_out.at[0], 6)]
     left_sent = share(0)
     for g in range(groups):
         links.received(returned[g])
@@ -334,10 +411,16 @@
         right_grad = own[chosen]
         for k in range(REACH):
             there = inside + (k + 1) < sizes["row"]
-            right_grad = right_grad + jnp.where(there, arrived[k, chosen].astype(F32), 0.0)
+            if k < MAXOFF:
+                got = arrived[k, chosen].astype(F32)
+            else:
+                got = unpacked_far(far_home, g * far)
+                there = jnp.logical_and(there, small >= width - disp)
+            right_grad = right_grad + jnp.where(there, got, 0.0)
         right_grad = right_grad.astype(BF16)
         grad_ref[1, chosen] = right_grad
         rounded[1, chosen] = right_grad.astype(F32)
+    saves.append(save(grad_ref.at[1], grad_out.at[1], 7))
     right_sent = share(1)
     pending += left_sent + right_sent
     empty = jnp.zeros((local, 9 * channels), F32)
@@ -380,15 +463,21 @@
             relayed[-1].start()
         for copy in relayed:
             copy.wait_recv()
+        saves.append(save(sum_ref, sum_out, 8))
         for copy in scattered + gathered + relayed:
             copy.wait_send()
     else:
         sum_ref[:local] = first
         sum_ref[local:] = second
+        saves.append(save(sum_ref, sum_out, 8))
     links.left(pending)
-
-
-def write_kernel(sum_ref, first_ref, second_ref):
+    for copy in saves:
+        copy.wait()
+
+
+def write_kernel(grad_ref, sum_ref, out_ref, first_ref, second_ref, sem):
+    copy = pltpu.make_async_copy(grad_ref, out_ref, sem)
+    copy.start()
     chans, pieces = sum_ref.shape[:2]
     channels = first_ref.shape[1]
     half = pieces // 2
@@ -404,6 +493,7 @@
         chosen = slice(t * channels, (t + 1) * channels)
         first_ref[t] = first[:, chosen]
         second_ref[8 - t] = second[chosen]
+    copy.wait()
 
 
 def body(sizes, layer_input, features, vol_target, offsets, w_first, w_second):
@@ -420,7 +510,9 @@
     rows = 2 * local // max(group, 2)
     views = (images, tile_w + 2, 3, channels, width)
     tile = (local, tile_w, width)
-    edge = (len(SIDES), images, channels, width)
+    image_per = min(width // (2 * images * tile_w), channels // 16)
+    grad_per = min(width // (2 * tile_w), local // 8)
+    far = vol_target.shape[0] * -(-size // (width // vol_target.shape[1]))
     count = 2 * REACH * vol_target.shape[0] + 2 + len(SIDES)
     count += images * ((chans - 1) + chans * (2 + len(SIDES))) + 3 * group
     if group:
@@ -430,12 +522,23 @@
     grad_features, summed = pl.pallas_call(
         functools.partial(whole_kernel, sizes, group),
         out_shape=[shape((2,) + tile, BF16), summed_shape],
-        in_specs=[vmem()] * 6,
-        out_specs=[vmem()] * 2,
+        in_specs=[vmem()] + [pl.BlockSpec(memory_space=pl.ANY)] * 5,
+        out_specs=[pl.BlockSpec(memory_space=pl.ANY)] * 2,
         scratch_shapes=[
+            scratch((2,) + tile, BF16),
+            scratch(summed_shape.shape, summed_shape.dtype),
+            scratch(features.shape, BF16),
+            scratch(vol_target.shape, BF16),
+            scratch(layer_input.shape, BF16),
+            scratch((3, 3, channels, channels), BF16),
+            scratch((3, 3, channels, channels), BF16),
+            scratch((far, tile_w, width), BF16),
+            scratch((far, tile_w, width), BF16),
+            scratch((far, tile_w, width), BF16),
+            scratch((far, tile_w, width), BF16),
             scratch((images, tile_w, channels, width), BF16),
-            scratch((images, channels, width), BF16),
-            scratch(edge, BF16),
+            scratch((channels // image_per, width), BF16),
+            scratch((len(SIDES), channels // image_per, width), BF16),
             scratch((2, images, channels, width), BF16),
             scratch(views, BF16),
             scratch((images, tile_w, local, width), BF16),
@@ -443,25 +546,26 @@
             scratch((local, 9 * channels), BF16),
             scratch((channels, tile_w, width), F32),
             scratch((channels, 9 * channels), F32),
-            scratch((REACH,) + tile, BF16),
+            scratch((MAXOFF,) + tile, BF16),
             scratch((size, tile_w, width), F32),
             scratch((size, tile_w, width), F32),
-            scratch((REACH,) + tile, BF16),
-            scratch((REACH,) + tile, BF16),
+            scratch((MAXOFF,) + tile, BF16),
+            scratch((MAXOFF,) + tile, BF16),
             scratch(tile, F32),
             scratch((2,) + tile, F32),
             scratch((2, chans, tile_w, local, width), BF16),
-            scratch((2, local, width), BF16),
-            scratch((2, len(SIDES), chans, local, width), BF16),
+            scratch((2, local // grad_per, width), BF16),
+            scratch((2, len(SIDES), chans, local // grad_per, width), BF16),
             scratch((2, 2, chans, local, width), BF16),
             scratch(views, BF16),
             scratch((max(group, 2), rows, 9 * channels), BF16),
             scratch((max(group, 2), rows, 9 * channels), BF16),
             dma((count,)),
             dma((count,)),
+            dma((9,)),
         ],
         compiler_params=pltpu.CompilerParams(
-            collective_id=0, has_side_effects=True, vmem_limit_bytes=48 * 1024 * 1024
+            collective_id=0, has_side_effects=True, vmem_limit_bytes=60 * 1024 * 1024
         ),
     )(
         offsets,
@@ -474,13 +578,14 @@
     if not group:
         summed = lax.all_gather(lax.psum(summed, ("row", "col")), "chan")
         summed = summed.reshape(chans, 2, local, 9 * channels)
-    first, second = pl.pallas_call(
+    grad_features, first, second = pl.pallas_call(
         write_kernel,
-        out_shape=[shape((9, channels, channels), F32)] * 2,
-        in_specs=[vmem()],
-        out_specs=[vmem()] * 2,
-        compiler_params=pltpu.CompilerParams(vmem_limit_bytes=16 * 1024 * 1024),
-    )(summed)
+        out_shape=[shape((2,) + tile, BF16)] + [shape((9, channels, channels), F32)] * 2,
+        in_specs=[pl.BlockSpec(memory_space=pl.ANY), vmem()],
+        out_specs=[pl.BlockSpec(memory_space=pl.ANY)] + [vmem()] * 2,
+        scratch_shapes=[dma],
+        compiler_params=pltpu.CompilerParams(vmem_limit_bytes=60 * 1024 * 1024),
+    )(grad_features, summed)
     first = first.reshape(3, 3, channels, channels).transpose(2, 3, 0, 1)
     second = second.reshape(3, 3, channels, channels).transpose(2, 3, 0, 1)
     return grad_features, first, second

time: 48 us -> 48.9 us (1.019)
  Pallas kernels: 41.1 us -> 47.5 us
  local copies, waits for them, and re-layouts: 5.29 us -> 0 us
    pallas_call x1, Pallas kernels: 0.93 us -> 6.81 us  [body(): pl.pallas_call(write_kernel, out_shape=[shape((2,) + tile, BF16)] + [shap...]
    unnamed x11 -> x0, local copies, waits for them, and re-layouts: 5.29 us -> none
    pallas_call x1, Pallas kernels: 40.1 us -> 40.7 us  [body(): pl.pallas_call(functools.partial(whole_kernel, sizes, group), out_shape=[...]
where the time goes in v3:
time: 48.9 us; the launch traced here: 48.8 us
  Pallas kernels  47.5 us (97%)
  between operations  1.29 us (3%)
    pallas_call x1, Pallas kernels, body(): pl.pallas_call(functools.partial(whole_kernel, sizes, group), out_shape=[...  40.7 us
    pallas_call x1, Pallas kernels, body(): pl.pallas_call(write_kernel, out_shape=[shape((2,) + tile, BF16)] + [shap...  6.81 us

profile of v3, /device:TPU:1, one launch (start us, length us, event | category | flops | bytes accessed | tf_op | source)
XLA Modules:
  0.0 48.8 jit_solution(15898496538154324839)
XLA Ops:
  1.3 40.7 %shard_map.85 = (bf16[2,32,8,128]{3,2,1,0:T(8,128)(2,1)}, bf16[2,8,8,576]{3,2,1,0:T(8,128)(2,1)}) custom-call(s32[1,1]{1,0:T(1,128)S(6)} %copy.9.offset_ref, bf16[2,32,8,128]{3,2,1,0:T(8,128)(2,1)} %features_hbm.1, bf16[4,40,8,128]{3,2,1,0:T(8,128)(2,1)} %target_hbm.1, bf16[2,64,8,128]{3,2,1,0:T(8,128)(2,1)} %image_hbm.1, bf16[3,3,64,64]{3,2,1,0:T(8,128)(2,1)} %bitcast.8, ...), custom_call_target="tpu_custom_call" | custom-call | tf_op jit(solution)/shard_map/pallas_call | solution.py:522
  42.0 6.8 %shard_map.86 = (bf16[2,32,8,128]{3,2,1,0:T(8,128)(2,1)}, f32[9,64,64]{2,1,0:T(8,128)}, f32[9,64,64]{2,1,0:T(8,128)}) custom-call(bf16[2,32,8,128]{3,2,1,0:T(8,128)(2,1)} %get-tuple-element.8.grad_ref, bf16[2,8,8,576]{3,2,1,0:T(8,128)(2,1)} %get-tuple-element.9.sum_ref), custom_call_target="tpu_custom_call" | custom-call | tf_op jit(solution)/shard_map/pallas_call | solution.py:581

commit v4 on v3

--- a/solution.py
+++ b/solution.py
@@ -84,7 +84,10 @@
             device = self.peer(-by, group)[1]
             pl.semaphore_signal(barrier, inc=1, device_id=device, device_id_type=MESH)
             count = count + 1
-        pl.semaphore_wait(barrier, count)
+        return count
+
+    def greeted(self, count):
+        pl.semaphore_wait(pltpu.get_barrier_semaphore(), count)
 
     def peer(self, by, group):
         cols = self.sizes["col"]
@@ -191,6 +194,11 @@
     backward = [{"row": -k} for k in range(1, REACH + 1)]
     with_chan = [{**move, "chan": c} for move in EDGE_MOVES + SIDE_MOVES for c in range(chans)]
     partners = [{"chan": c} for c in range(1, chans)]
+    met = with_chan + partners
+    if direct:
+        met = [move for move in met if move["chan"]]
+    else:
+        met = met + forward + backward
     loads = [
         pltpu.make_async_copy(src, dst, load_sem.at[i])
         for i, (src, dst) in enumerate([
@@ -204,6 +212,7 @@
     ]
     for load in loads:
         load.start()
+    expected = links.greet(met, group)
     pending = []
     lanes = lane_index((channels, width))
     small = lane_index((tile_w, width))
@@ -233,42 +242,48 @@
     loads[0].wait()
     for g in range(groups):
         packed_far(features_ref[1, g * size : (g + 1) * size].astype(F32), far_out, g * far)
-    links.greet(forward + backward + with_chan + partners, group)
-
-    def parts_of(g):
-        return pl.ds(g * size, size)
-
-    fetched = []
-    for g in range(groups):
-        fetched.append([
-            links.send(
-                forward[k], features_ref.at[1, parts_of(g)], window.at[k, parts_of(g)]
-            )
-            for k in range(MAXOFF)
-        ])
-        fetched[-1].append(
-            links.send(forward[MAXOFF], far_out.at[far_of(g)], far_in.at[far_of(g)])
-        )
-        pending += fetched[-1]
 
     loads[1].wait()
     for n in range(images):
         turned[...] = image_ref[n].astype(F32)
         for x in range(tile_w):
             image[n, x] = turned[:, x, :].astype(BF16)
-    border = [
-        links.send(move, image.at[:, x], image_side.at[side])
-        for side, (x, move) in enumerate(zip((tile_w - 1, 0), SIDE_MOVES))
-    ]
     count = images * tile_w
     image_per = channels // image_pack.shape[0]
     image_pack[...] = packed_edges(
         [image[n, x].astype(F32) for n in range(images) for x in range(tile_w)], image_per
     ).astype(BF16)
+    links.greeted(expected)
+
+    def parts_of(g):
+        return pl.ds(g * size, size)
+
+    fetched = {}
+    chunk = groups // 2 if groups % 2 == 0 else groups
+
+    def fetch(g):
+        chosen = pl.ds(g * size, chunk * size)
+        far_chosen = pl.ds(g * far, chunk * far)
+        fetched[g] = [
+            links.send(move, features_ref.at[1, chosen], window.at[k, chosen])
+            for k, move in enumerate(forward[:MAXOFF])
+        ]
+        fetched[g].append(
+            links.send(forward[MAXOFF], far_out.at[far_chosen], far_in.at[far_chosen])
+        )
+        pending.extend(fetched[g])
+
+    fetch(0)
+    border = [
+        links.send(move, image.at[:, x], image_side.at[side])
+        for side, (x, move) in enumerate(zip((tile_w - 1, 0), SIDE_MOVES))
+    ]
     border += [
         links.send(move, image_pack, image_edges.at[j]) for j, move in enumerate(EDGE_MOVES)
     ]
     pending += border
+    for g in range(chunk, groups, chunk):
+        fetch(g)
 
     loads[2].wait()
     loads[3].wait()
@@ -289,11 +304,6 @@
             lambda j: [image_edges[j].astype(F32)],
             tile_w, lanes, image_per, count, n * tile_w,
         )
-    for n in range(images):
-        for x in range(tile_w):
-            view = image_views[n, x : x + 3].reshape(9 * channels, width)
-            total = jnp.dot(w1[...], view, preferred_element_type=F32)
-            hidden_s[n, x] = jnp.maximum(total, 0.0).astype(BF16)
 
     loads[4].wait()
     loads[5].wait()
@@ -305,7 +315,7 @@
     ]
     returned = []
     for g in range(groups):
-        links.received(fetched[g])
+        links.received(fetched.get(g, []))
         chosen = parts_of(g)
         main = jnp.where(main_in[0], features_ref[1, chosen].astype(F32), 0.0)
         spill = jnp.zeros_like(main)
@@ -405,6 +415,11 @@
 
     saves = [save(grad_ref.at[0], grad_out.at[0], 6)]
     left_sent = share(0)
+    for n in range(images):
+        for x in range(tile_w):
+            view = image_views[n, x : x + 3].reshape(9 * channels, width)
+            total = jnp.dot(w1[...], view, preferred_element_type=F32)
+            hidden_s[n, x] = jnp.maximum(total, 0.0).astype(BF16)
     for g in range(groups):
         links.received(returned[g])
         chosen = parts_of(g)
@@ -443,6 +458,7 @@
             rank, device = links.peer(by, group)
             scattered.append(links.copy(part.at[rank], parts.at[by - 1], device))
             scattered[-1].start()
+        links.left(pending)
         me = links.peer(0, group)[0]
         total = part[me].astype(F32)
         for by in range(1, group):
@@ -470,14 +486,13 @@
         sum_ref[:local] = first
         sum_ref[local:] = second
         saves.append(save(sum_ref, sum_out, 8))
-    links.left(pending)
+        links.left(pending)
     for copy in saves:
         copy.wait()
 
 
-def write_kernel(grad_ref, sum_ref, out_ref, first_ref, second_ref, sem):
-    copy = pltpu.make_async_copy(grad_ref, out_ref, sem)
-    copy.start()
+def write_kernel(grad_ref, sum_ref, out_ref, first_ref, second_ref):
+    out_ref[...] = grad_ref[...]
     chans, pieces = sum_ref.shape[:2]
     channels = first_ref.shape[1]
     half = pieces // 2
@@ -493,7 +508,6 @@
         chosen = slice(t * channels, (t + 1) * channels)
         first_ref[t] = first[:, chosen]
         second_ref[8 - t] = second[chosen]
-    copy.wait()
 
 
 def body(sizes, layer_input, features, vol_target, offsets, w_first, w_second):
@@ -581,9 +595,8 @@
     grad_features, first, second = pl.pallas_call(
         write_kernel,
         out_shape=[shape((2,) + tile, BF16)] + [shape((9, channels, channels), F32)] * 2,
-        in_specs=[pl.BlockSpec(memory_space=pl.ANY), vmem()],
-        out_specs=[pl.BlockSpec(memory_space=pl.ANY)] + [vmem()] * 2,
-        scratch_shapes=[dma],
+        in_specs=[vmem()] * 2,
+        out_specs=[vmem()] * 3,
         compiler_params=pltpu.CompilerParams(vmem_limit_bytes=60 * 1024 * 1024),
     )(grad_features, summed)
     first = first.reshape(3, 3, channels, channels).transpose(2, 3, 0, 1)

time: 48.9 us -> 41.6 us (0.85)
  Pallas kernels: 47.5 us -> 40.2 us
    pallas_call x1, Pallas kernels: 6.81 us -> 1.94 us  [body(): pl.pallas_call(write_kernel, out_shape=[shape((2,) + tile, BF16)] + [shap...]
    pallas_call x1, Pallas kernels: 40.7 us -> 38.2 us  [body(): pl.pallas_call(functools.partial(whole_kernel, sizes, group), out_shape=[...]
where the time goes in v4:
time: 41.6 us; the launch traced here: 41.5 us
  Pallas kernels  40.2 us (97%)
  between operations  1.29 us (3%)
    pallas_call x1, Pallas kernels, body(): pl.pallas_call(functools.partial(whole_kernel, sizes, group), out_shape=[...  38.2 us
    pallas_call x1, Pallas kernels, body(): pl.pallas_call(write_kernel, out_shape=[shape((2,) + tile, BF16)] + [shap...  1.94 us

profile of v4, /device:TPU:1, one launch (start us, length us, event | category | flops | bytes accessed | tf_op | source)
XLA Modules:
  0.0 41.5 jit_solution(7720080337053925316)
XLA Ops:
  1.3 38.2 %shard_map.85 = (bf16[2,32,8,128]{3,2,1,0:T(8,128)(2,1)}, bf16[2,8,8,576]{3,2,1,0:T(8,128)(2,1)}) custom-call(s32[1,1]{1,0:T(1,128)S(6)} %copy.9.offset_ref, bf16[2,32,8,128]{3,2,1,0:T(8,128)(2,1)} %features_hbm.1, bf16[4,40,8,128]{3,2,1,0:T(8,128)(2,1)} %target_hbm.1, bf16[2,64,8,128]{3,2,1,0:T(8,128)(2,1)} %image_hbm.1, bf16[3,3,64,64]{3,2,1,0:T(8,128)(2,1)} %bitcast.8, ...), custom_call_target="tpu_custom_call" | custom-call | tf_op jit(solution)/shard_map/pallas_call | solution.py:536
  39.5 1.9 %shard_map.86 = (bf16[2,32,8,128]{3,2,1,0:T(8,128)(2,1)}, f32[9,64,64]{2,1,0:T(8,128)}, f32[9,64,64]{2,1,0:T(8,128)}) custom-call(bf16[2,32,8,128]{3,2,1,0:T(8,128)(2,1)} %get-tuple-element.8.grad_ref, bf16[2,8,8,576]{3,2,1,0:T(8,128)(2,1)} %get-tuple-element.9.sum_ref), custom_call_target="tpu_custom_call" | custom-call | tf_op jit(solution)/shard_map/pallas_call | solution.py:595

commit v5 on v4

--- a/solution.py
+++ b/solution.py
@@ -259,11 +259,11 @@
         return pl.ds(g * size, size)
 
     fetched = {}
-    chunk = groups // 2 if groups % 2 == 0 else groups
-
-    def fetch(g):
-        chosen = pl.ds(g * size, chunk * size)
-        far_chosen = pl.ds(g * far, chunk * far)
+    starts = sorted({min(at, groups) for at in (0, 1, 2, groups)})
+
+    def fetch(g, after):
+        chosen = pl.ds(g * size, (after - g) * size)
+        far_chosen = pl.ds(g * far, (after - g) * far)
         fetched[g] = [
             links.send(move, features_ref.at[1, chosen], window.at[k, chosen])
             for k, move in enumerate(forward[:MAXOFF])
@@ -273,7 +273,7 @@
         )
         pending.extend(fetched[g])
 
-    fetch(0)
+    fetch(*starts[:2])
     border = [
         links.send(move, image.at[:, x], image_side.at[side])
         for side, (x, move) in enumerate(zip((tile_w - 1, 0), SIDE_MOVES))
@@ -282,8 +282,8 @@
         links.send(move, image_pack, image_edges.at[j]) for j, move in enumerate(EDGE_MOVES)
     ]
     pending += border
-    for g in range(chunk, groups, chunk):
-        fetch(g)
+    for g, after in zip(starts[1:], starts[2:]):
+        fetch(g, after)
 
     loads[2].wait()
     loads[3].wait()
@@ -328,7 +328,7 @@
         spill_s[...] = spill
 
         def step(t, state, g=g, chosen=chosen):
-            left_grad, main_grad, spill_grad = state
+            left_grad, total, early = state
             left = features_ref[0, chosen].astype(F32)
             for j in range(8):
                 d = t * 8 + j
@@ -338,12 +338,15 @@
                 weighted = (volume - target_ref[g, d].astype(F32)) * inv
                 left_grad = left_grad + weighted * shifted
                 back = pltpu.roll(weighted * left, lax.rem(width - d, width), 2)
-                main_grad = main_grad + jnp.where(keep, back, 0.0)
-                spill_grad = spill_grad + jnp.where(keep, 0.0, back)
-            return left_grad, main_grad, spill_grad
+                early = jnp.where(small == width - d, total, early)
+                total = total + back
+            return left_grad, total, early
 
         zero = jnp.zeros((size, tile_w, width), F32)
-        left_grad, main_grad, spill_grad = lax.fori_loop(0, disp // 8, step, (zero, zero, zero))
+        left_grad, total, early = lax.fori_loop(0, disp // 8, step, (zero, zero, zero))
+        both = small > width - disp
+        main_grad = jnp.where(both, early, total)
+        spill_grad = jnp.where(both, total - early, 0.0)
         for k in range(1, REACH + 1):
             piece = jnp.where(spill_in[k - 1], spill_grad, 0.0)
             if k < REACH:
@@ -398,13 +401,13 @@
             lambda j: [grad_edges[n, j, c].astype(F32) for c in range(chans)],
             tile_w, lanes, grad_per, tile_w, 0,
         )
-        for x in range(tile_w):
-            view = grad_views[n, x : x + 3].reshape(9 * channels, width)
-            hidden = hidden_s[n, x]
+        for at in range(tile_w // abreast_rows):
+            view = view_of(grad_views, n, at)
+            hidden = hidden_s[n, at]
             total = jnp.dot(w2[...], view, preferred_element_type=F32)
             hidden_grad = jnp.where(hidden.astype(F32) > 0, total, 0.0).astype(BF16)
             second += lax.dot_general(hidden, view, contract, preferred_element_type=F32)
-            seen = image_views[n, x : x + 3].reshape(9 * channels, width)
+            seen = view_of(image_views, n, at)
             first += lax.dot_general(hidden_grad, seen, contract, preferred_element_type=F32)
         return first, second
 
@@ -415,11 +418,18 @@
 
     saves = [save(grad_ref.at[0], grad_out.at[0], 6)]
     left_sent = share(0)
+    abreast_rows = hidden_s.shape[3] // width
+
+    def view_of(views, n, at):
+        rows = range(at * abreast_rows, (at + 1) * abreast_rows)
+        return jnp.concatenate(
+            [views[n, x : x + 3].reshape(9 * channels, width) for x in rows], axis=1
+        )
+
     for n in range(images):
-        for x in range(tile_w):
-            view = image_views[n, x : x + 3].reshape(9 * channels, width)
-            total = jnp.dot(w1[...], view, preferred_element_type=F32)
-            hidden_s[n, x] = jnp.maximum(total, 0.0).astype(BF16)
+        for at in range(tile_w // abreast_rows):
+            total = jnp.dot(w1[...], view_of(image_views, n, at), preferred_element_type=F32)
+            hidden_s[n, at] = jnp.maximum(total, 0.0).astype(BF16)
     for g in range(groups):
         links.received(returned[g])
         chosen = parts_of(g)
@@ -524,6 +534,7 @@
     rows = 2 * local // max(group, 2)
     views = (images, tile_w + 2, 3, channels, width)
     tile = (local, tile_w, width)
+    pair = 2 if tile_w % 2 == 0 else 1
     image_per = min(width // (2 * images * tile_w), channels // 16)
     grad_per = min(width // (2 * tile_w), local // 8)
     far = vol_target.shape[0] * -(-size // (width // vol_target.shape[1]))
@@ -555,7 +566,7 @@
             scratch((len(SIDES), channels // image_per, width), BF16),
             scratch((2, images, channels, width), BF16),
             scratch(views, BF16),
-            scratch((images, tile_w, local, width), BF16),
+            scratch((images, tile_w // pair, local, pair * width), BF16),
             scratch((local, 9 * channels), BF16),
             scratch((local, 9 * channels), BF16),
             scratch((channels, tile_w, width), F32),

time: 41.6 us -> 40.1 us (0.964)
  Pallas kernels: 40.2 us -> 38.6 us
    pallas_call x1, Pallas kernels: 38.2 us -> 36.7 us  [body(): pl.pallas_call(functools.partial(whole_kernel, sizes, group), out_shape=[...]
where the time goes in v5:
time: 40.1 us; the launch traced here: 39.9 us
  Pallas kernels  38.6 us (96%)
  between operations  1.29 us (3%)
    pallas_call x1, Pallas kernels, body(): pl.pallas_call(functools.partial(whole_kernel, sizes, group), out_shape=[...  36.7 us
    pallas_call x1, Pallas kernels, body(): pl.pallas_call(write_kernel, out_shape=[shape((2,) + tile, BF16)] + [shap...  1.94 us

profile of v5, /device:TPU:1, one launch (start us, length us, event | category | flops | bytes accessed | tf_op | source)
XLA Modules:
  0.0 39.9 jit_solution(9662153551342818203)
XLA Ops:
  1.3 36.7 %shard_map.85 = (bf16[2,32,8,128]{3,2,1,0:T(8,128)(2,1)}, bf16[2,8,8,576]{3,2,1,0:T(8,128)(2,1)}) custom-call(s32[1,1]{1,0:T(1,128)S(6)} %copy.9.offset_ref, bf16[2,32,8,128]{3,2,1,0:T(8,128)(2,1)} %features_hbm.1, bf16[4,40,8,128]{3,2,1,0:T(8,128)(2,1)} %target_hbm.1, bf16[2,64,8,128]{3,2,1,0:T(8,128)(2,1)} %image_hbm.1, bf16[3,3,64,64]{3,2,1,0:T(8,128)(2,1)} %bitcast.8, ...), custom_call_target="tpu_custom_call" | custom-call | tf_op jit(solution)/shard_map/pallas_call | solution.py:547
  38.0 1.9 %shard_map.86 = (bf16[2,32,8,128]{3,2,1,0:T(8,128)(2,1)}, f32[9,64,64]{2,1,0:T(8,128)}, f32[9,64,64]{2,1,0:T(8,128)}) custom-call(bf16[2,32,8,128]{3,2,1,0:T(8,128)(2,1)} %get-tuple-element.8.grad_ref, bf16[2,8,8,576]{3,2,1,0:T(8,128)(2,1)} %get-tuple-element.9.sum_ref), custom_call_target="tpu_custom_call" | custom-call | tf_op jit(solution)/shard_map/pallas_call | solution.py:606

commit v6 on v5

--- a/solution.py
+++ b/solution.py
@@ -243,16 +243,6 @@
     for g in range(groups):
         packed_far(features_ref[1, g * size : (g + 1) * size].astype(F32), far_out, g * far)
 
-    loads[1].wait()
-    for n in range(images):
-        turned[...] = image_ref[n].astype(F32)
-        for x in range(tile_w):
-            image[n, x] = turned[:, x, :].astype(BF16)
-    count = images * tile_w
-    image_per = channels // image_pack.shape[0]
-    image_pack[...] = packed_edges(
-        [image[n, x].astype(F32) for n in range(images) for x in range(tile_w)], image_per
-    ).astype(BF16)
     links.greeted(expected)
 
     def parts_of(g):
@@ -274,6 +264,19 @@
         pending.extend(fetched[g])
 
     fetch(*starts[:2])
+    for g, after in zip(starts[1:], starts[2:]):
+        fetch(g, after)
+
+    loads[1].wait()
+    for n in range(images):
+        turned[...] = image_ref[n].astype(F32)
+        for x in range(tile_w):
+            image[n, x] = turned[:, x, :].astype(BF16)
+    count = images * tile_w
+    image_per = channels // image_pack.shape[0]
+    image_pack[...] = packed_edges(
+        [image[n, x].astype(F32) for n in range(images) for x in range(tile_w)], image_per
+    ).astype(BF16)
     border = [
         links.send(move, image.at[:, x], image_side.at[side])
         for side, (x, move) in enumerate(zip((tile_w - 1, 0), SIDE_MOVES))
@@ -282,8 +285,6 @@
         links.send(move, image_pack, image_edges.at[j]) for j, move in enumerate(EDGE_MOVES)
     ]
     pending += border
-    for g, after in zip(starts[1:], starts[2:]):
-        fetch(g, after)
 
     loads[2].wait()
     loads[3].wait()
@@ -294,16 +295,6 @@
     flipped = jnp.concatenate([w2_ref[2 - a, 2 - b].astype(F32) for a, b in taps], axis=0)
     turned_w[...] = flipped.T
     w2[...] = turned_w[mine].astype(BF16)
-
-    links.received(border)
-    for n in range(images):
-        fill_views(
-            image_views, links, n,
-            lambda x, n=n: image[n, x].astype(F32),
-            lambda side, n=n: image_side[side, n].astype(F32),
-            lambda j: [image_edges[j].astype(F32)],
-            tile_w, lanes, image_per, count, n * tile_w,
-        )
 
     loads[4].wait()
     loads[5].wait()
@@ -426,10 +417,22 @@
             [views[n, x : x + 3].reshape(9 * channels, width) for x in rows], axis=1
         )
 
+    links.received(border)
     for n in range(images):
+        fill_views(
+            image_views, links, n,
+            lambda x, n=n: image[n, x].astype(F32),
+            lambda side, n=n: image_side[side, n].astype(F32),
+            lambda j: [image_edges[j].astype(F32)],
+            tile_w, lanes, image_per, count, n * tile_w,
+        )
+
+    def recompute_hidden(n):
         for at in range(tile_w // abreast_rows):
             total = jnp.dot(w1[...], view_of(image_views, n, at), preferred_element_type=F32)
             hidden_s[n, at] = jnp.maximum(total, 0.0).astype(BF16)
+
+    recompute_hidden(0)
     for g in range(groups):
         links.received(returned[g])
         chosen = parts_of(g)
@@ -451,6 +454,7 @@
     empty = jnp.zeros((local, 9 * channels), F32)
     links.received(left_sent)
     first, second = gradients(0, empty, empty)
+    recompute_hidden(1)
     links.received(right_sent)
     first, second = gradients(1, first, second)
     pixels = images * tile_w * sizes["col"] * width * sizes["row"]

time: 40.1 us -> 40 us (level)
  no operation moved by 1% of the time
where the time goes in v6:
time: 40 us; the launch traced here: 39.8 us
  Pallas kernels  38.5 us (96%)
  between operations  1.29 us (3%)
    pallas_call x1, Pallas kernels, body(): pl.pallas_call(functools.partial(whole_kernel, sizes, group), out_shape=[...  36.6 us
    pallas_call x1, Pallas kernels, body(): pl.pallas_call(write_kernel, out_shape=[shape((2,) + tile, BF16)] + [shap...  1.94 us

profile of v6, /device:TPU:1, one launch (start us, length us, event | category | flops | bytes accessed | tf_op | source)
XLA Modules:
  0.0 39.8 jit_solution(12851992898226751795)
XLA Ops:
  1.3 36.6 %shard_map.85 = (bf16[2,32,8,128]{3,2,1,0:T(8,128)(2,1)}, bf16[2,8,8,576]{3,2,1,0:T(8,128)(2,1)}) custom-call(s32[1,1]{1,0:T(1,128)S(6)} %copy.9.offset_ref, bf16[2,32,8,128]{3,2,1,0:T(8,128)(2,1)} %features_hbm.1, bf16[4,40,8,128]{3,2,1,0:T(8,128)(2,1)} %target_hbm.1, bf16[2,64,8,128]{3,2,1,0:T(8,128)(2,1)} %image_hbm.1, bf16[3,3,64,64]{3,2,1,0:T(8,128)(2,1)} %bitcast.8, ...), custom_call_target="tpu_custom_call" | custom-call | tf_op jit(solution)/shard_map/pallas_call | solution.py:551
  37.9 1.9 %shard_map.86 = (bf16[2,32,8,128]{3,2,1,0:T(8,128)(2,1)}, f32[9,64,64]{2,1,0:T(8,128)}, f32[9,64,64]{2,1,0:T(8,128)}) custom-call(bf16[2,32,8,128]{3,2,1,0:T(8,128)(2,1)} %get-tuple-element.8.grad_ref, bf16[2,8,8,576]{3,2,1,0:T(8,128)(2,1)} %get-tuple-element.9.sum_ref), custom_call_target="tpu_custom_call" | custom-call | tf_op jit(solution)/shard_map/pallas_call | solution.py:610

commit v7 on v6

--- a/solution.py
+++ b/solution.py
@@ -239,9 +239,6 @@
     def far_of(g):
         return pl.ds(g * far, far)
 
-    loads[0].wait()
-    for g in range(groups):
-        packed_far(features_ref[1, g * size : (g + 1) * size].astype(F32), far_out, g * far)
 
     links.greeted(expected)
 
@@ -253,19 +250,25 @@
 
     def fetch(g, after):
         chosen = pl.ds(g * size, (after - g) * size)
-        far_chosen = pl.ds(g * far, (after - g) * far)
         fetched[g] = [
-            links.send(move, features_ref.at[1, chosen], window.at[k, chosen])
+            links.send(move, features_hbm.at[1, chosen], window.at[k, chosen])
             for k, move in enumerate(forward[:MAXOFF])
         ]
+
+    def fetch_far(g, after):
+        far_chosen = pl.ds(g * far, (after - g) * far)
         fetched[g].append(
             links.send(forward[MAXOFF], far_out.at[far_chosen], far_in.at[far_chosen])
         )
         pending.extend(fetched[g])
 
-    fetch(*starts[:2])
-    for g, after in zip(starts[1:], starts[2:]):
+    for g, after in zip(starts, starts[1:]):
         fetch(g, after)
+    loads[0].wait()
+    for g in range(groups):
+        packed_far(features_ref[1, g * size : (g + 1) * size].astype(F32), far_out, g * far)
+    for g, after in zip(starts, starts[1:]):
+        fetch_far(g, after)
 
     loads[1].wait()
     for n in range(images):

time: 40 us -> 41.4 us (1.035)
  Pallas kernels: 38.5 us -> 40 us
    pallas_call x1, Pallas kernels: 36.6 us -> 38 us  [body(): pl.pallas_call(functools.partial(whole_kernel, sizes, group), out_shape=[...]
where the time goes in v7:
time: 41.4 us; the launch traced here: 41.2 us
  Pallas kernels  40 us (97%)
  between operations  1.29 us (3%)
    pallas_call x1, Pallas kernels, body(): pl.pallas_call(functools.partial(whole_kernel, sizes, group), out_shape=[...  38 us
    pallas_call x1, Pallas kernels, body(): pl.pallas_call(write_kernel, out_shape=[shape((2,) + tile, BF16)] + [shap...  1.94 us

profile of v7, /device:TPU:1, one launch (start us, length us, event | category | flops | bytes accessed | tf_op | source)
XLA Modules:
  0.0 41.2 jit_solution(1874090861353764878)
XLA Ops:
  1.3 38.0 %shard_map.85 = (bf16[2,32,8,128]{3,2,1,0:T(8,128)(2,1)}, bf16[2,8,8,576]{3,2,1,0:T(8,128)(2,1)}) custom-call(s32[1,1]{1,0:T(1,128)S(6)} %copy.9.offset_ref, bf16[2,32,8,128]{3,2,1,0:T(8,128)(2,1)} %features_hbm.1, bf16[4,40,8,128]{3,2,1,0:T(8,128)(2,1)} %target_hbm.1, bf16[2,64,8,128]{3,2,1,0:T(8,128)(2,1)} %image_hbm.1, bf16[3,3,64,64]{3,2,1,0:T(8,128)(2,1)} %bitcast.8, ...), custom_call_target="tpu_custom_call" | custom-call | tf_op jit(solution)/shard_map/pallas_call | solution.py:554
  39.3 1.9 %shard_map.86 = (bf16[2,32,8,128]{3,2,1,0:T(8,128)(2,1)}, f32[9,64,64]{2,1,0:T(8,128)}, f32[9,64,64]{2,1,0:T(8,128)}) custom-call(bf16[2,32,8,128]{3,2,1,0:T(8,128)(2,1)} %get-tuple-element.8.grad_ref, bf16[2,8,8,576]{3,2,1,0:T(8,128)(2,1)} %get-tuple-element.9.sum_ref), custom_call_target="tpu_custom_call" | custom-call | tf_op jit(solution)/shard_map/pallas_call | solution.py:613
